TPU v7x, 256 devices: a whole 4x4x8 slice. The times are simulated.
256 devices in a mesh: dp: 16 (over y_lo, x, core), tensor: 16 (over z, y_hi).
Axes of the slice: x: 4, y: 4 (y_hi: 2, y_lo: 2; y = y_hi * 2 + y_lo), z: 8, core: 2. Of those that a mesh axis runs over, the one named last changes fastest.
Arguments:
- acts: bfloat16 [8192, 2048], P('dp', 'tensor'), may hold values from -6 to 6
- out_grads: bfloat16 [8192, 8192], P('dp', 'tensor'), may hold values from -6 to 6
- basis_out: bfloat16 [8192, 8192], P('tensor'), may hold values from -0.0625 to 0.0625
- basis_in: bfloat16 [2048, 2048], P('tensor'), may hold values from -0.125 to 0.125
- slot_sequence: int32 [32], replicated, may hold values from 0 to 31, each once
- seq_lengths: int32 [32], replicated, may hold values from 1 to 256, 5120 in all
Outputs:
- eigenvalues: float32 [8192, 2048], P('tensor', 'dp')
Inputs may be any that keep to these rules, and one draw needn't show every extreme that they name: `slot_sequence`: every sequence number appears exactly once. `seq_lengths`: the largest count is exactly 256.
All inputs are finite; a program needn't handle non-finite values.
Results may differ from a plain program's by a relative error of at most 0.0018.
Values may be sent and summed in bfloat16 or wider, within the bound.
A program may use at most 128 MiB of HBM per device.

v0:
```python
import jax
import jax.numpy as jnp
from jax import lax
from jax.sharding import PartitionSpec as P

LEN = 256


def shards(acts, out_grads, basis_out, basis_in, slot_sequence, seq_lengths):
    tok_rows = acts.shape[0]
    local_seqs = tok_rows // LEN
    seq_total = seq_lengths.shape[0]
    group_index = lax.axis_index("dp")
    slot_ids = group_index * local_seqs + jnp.arange(local_seqs, dtype=jnp.int32)
    seq_numbers = jnp.arange(seq_total, dtype=jnp.int32)
    which_seq = jnp.sum(
        jnp.where(slot_ids[:, None] == seq_numbers[None, :], slot_sequence[None, :], 0), axis=1
    )
    slot_counts = jnp.sum(
        jnp.where(which_seq[:, None] == seq_numbers[None, :], seq_lengths[None, :], 0), axis=1
    )
    row_counts = jnp.repeat(slot_counts, LEN)
    positions = jnp.arange(tok_rows, dtype=jnp.int32) % LEN
    valid_mask = positions < row_counts
    masked = jnp.where(valid_mask[:, None], out_grads, jnp.zeros_like(out_grads))
    rot_sums = lax.psum_scatter(
        jnp.einsum("oi,to->it", basis_out, masked, preferred_element_type=jnp.float32),
        "tensor",
        scatter_dimension=0,
        tiled=True,
    )
    rot_grads = rot_sums.astype(jnp.bfloat16)
    whole_acts = lax.all_gather(acts, "tensor", axis=1, tiled=True)
    rot_acts = jnp.dot(
        whole_acts,
        lax.all_gather(basis_in, "tensor", axis=0, tiled=True),
        preferred_element_type=jnp.float32,
    ).astype(jnp.bfloat16)
    squares = jnp.zeros((rot_grads.shape[0], rot_acts.shape[1]), jnp.float32)
    for slot_pos in range(local_seqs):
        grad_slot = rot_grads[:, slot_pos * LEN : (slot_pos + 1) * LEN]
        act_slot = rot_acts[slot_pos * LEN : (slot_pos + 1) * LEN]
        rotated = jnp.dot(grad_slot, act_slot, preferred_element_type=jnp.float32)
        squares = squares + rotated * rotated
    summed = lax.psum_scatter(squares, "dp", scatter_dimension=1, tiled=True)
    return summed / (seq_total * LEN)


def solution(mesh):
    return jax.shard_map(
        shards,
        mesh=mesh,
        in_specs=(
            P("dp", "tensor"),
            P("dp", "tensor"),
            P("tensor", None),
            P("tensor", None),
            P(),
            P(),
        ),
        out_specs=P("tensor", "dp"),
        check_vma=False,
    )
```

profile of v0, /device:TPU:1, one launch (start us, length us, event | category | flops | bytes accessed | tf_op | source)
XLA Modules:
  0.0 600.9 jit_solution(11152141464719970402)
XLA Ops:
  6.5 0.0 all-gather.3.cloned.1.call-start
  6.5 0.7 all-gather.3.cloned.1.call-update
  7.3 0.0 all-gather.5.cloned.1.call-start
  7.3 0.7 all-gather.5.cloned.1.call-update
  8.0 0.0 reduce-scatter.3.cloned.1.call-start
  8.1 0.8 fusion.12
  8.9 0.8 fusion.13
  9.7 0.1 broadcast_bitcast_fusion
  9.8 13.9 %convolution_bitcast_fusion = f32[8192,512]{0,1:T(8,128)} fusion(bf16[512,8192]{1,0:T(8,128)(2,1)} %param.8, bf16[512,512]{1,0:T(8,128)(2,1)} %param.7, pred[512]{0:T(512)(128)(4,1)S(1)} %fusion.8), kind=kOutput, calls=%fused_computation | convolution fusion | flops 4295229440 | bytes 25690624 | tf_op jit(solution)/shard_map/oi,to->it/dot_general | solution.py:27
  23.7 0.0 reduce-scatter.3.cloned.1.call-update
  23.7 0.0 reduce-scatter.5.cloned.1.call-start
  23.8 71.8 %all-gather.3.cloned.1.call-done = bf16[512,2048]{1,0:T(8,128)(2,1)} async-done(((bf16[512,128]{1,0:T(8,128)(2,1)}), bf16[512,2048]{1,0:T(8,128)(2,1)}) %all-gather.3.cloned.1.call-update) | async-done | bytes 2097168 | tf_op jit(solution)/shard_map/all_gather | solution.py:33
  95.6 137.7 %all-gather.5.cloned.1.call-done = bf16[2048,2048]{1,0:T(8,128)(2,1)} async-done(((bf16[128,2048]{1,0:T(8,128)(2,1)}), bf16[2048,2048]{1,0:T(8,128)(2,1)}) %all-gather.5.cloned.1.call-update) | async-done | bytes 8388624 | tf_op jit(solution)/shard_map/all_gather | solution.py:36
  233.3 8.5 %convolution_convert_fusion = bf16[512,2048]{1,0:T(8,128)(2,1)S(1)} fusion(bf16[512,2048]{1,0:T(8,128)(2,1)} %all-gather.3.cloned.1.call-done, bf16[2048,2048]{1,0:T(8,128)(2,1)} %all-gather.5.cloned.1.call-done), kind=kOutput, calls=%fused_computation.2 | convolution fusion | flops 4296015872 | bytes 12582912 | tf_op jit(solution)/shard_map/dot_general | solution.py:34
  241.8 282.5 %reduce-scatter.3.cloned.1.call-done = f32[512,512]{0,1:T(8,128)} async-done(((f32[8192,512]{0,1:T(8,128)}), f32[512,512]{0,1:T(8,128)}) %reduce-scatter.3.cloned.1.call-update) | async-done | bytes 1048592 | tf_op jit(solution)/shard_map/reduce_scatter | solution.py:26
  524.3 1.3 convert_element_type.6
  525.6 0.7 fusion.1
  526.3 2.7 multiply_add_fusion
  529.0 0.0 reduce-scatter.5.cloned.1.call-update
  529.0 63.6 %reduce-scatter.5.cloned.1.call-done = f32[512,128]{1,0:T(8,128)} async-done(((f32[512,2048]{1,0:T(8,128)}), f32[512,128]{1,0:T(8,128)}) %reduce-scatter.5.cloned.1.call-update) | async-done | bytes 262160 | tf_op jit(solution)/shard_map/reduce_scatter | solution.py:45
  592.7 1.7 broadcast_multiply_fusion
  (3 shorter events, 0.0 us)
Async XLA Ops:
  6.5 89.0 %all-gather.3.cloned.1.call-start = ((), (), s32[]{:S(2)}) async-start(), calls=%async_computation.3 | async-start | bytes 2228224 | tf_op jit(solution)/shard_map/all_gather | solution.py:33
  7.3 226.0 %all-gather.5.cloned.1.call-start = ((), (), s32[]{:S(2)}) async-start(), calls=%async_computation.4 | async-start | bytes 8912896 | tf_op jit(solution)/shard_map/all_gather | solution.py:36
  8.0 516.3 %reduce-scatter.3.cloned.1.call-start = ((), (), s32[]{:S(2)}) async-start(), calls=%async_computation.2 | async-start | bytes 17825792 | tf_op jit(solution)/shard_map/reduce_scatter | solution.py:26
  23.7 569.0 %reduce-scatter.5.cloned.1.call-start = ((), (), s32[]{:S(2)}) async-start(), calls=%async_computation.5 | async-start | bytes 4456448 | tf_op jit(solution)/shard_map/reduce_scatter | solution.py:45
Sparse Core Ops, SparseCore 0:
  9.8 85.6 all-gather.2
  98.2 135.0 all-gather.4
  237.4 286.8 reduce-scatter.2
  529.2 63.4 reduce-scatter.4
where the time goes:
time: 603 us; the launch traced here: 601 us
  waiting for transfers between devices  557 us (92%)
  matrix products  25.8 us (4%)
  between operations  13.2 us (2%)
    reduce_scatter x1, waiting for transfers between devices, shards(): lax.psum_scatter(jnp.einsum('oi,to->it', basis_out, masked, preferred_ele...  282 us
    all_gather x1, waiting for transfers between devices, shards(): lax.all_gather(basis_in, 'tensor', axis=0, tiled=True)  138 us
    all_gather x1, waiting for transfers between devices, shards(): whole_acts = lax.all_gather(acts, 'tensor', axis=1, tiled=True)  71.8 us
    reduce_scatter x1, waiting for transfers between devices, shards(): summed = lax.psum_scatter(squares, 'dp', scatter_dimension=1, tiled=True)  63.6 us
    dot_general x1, matrix products, shards(): jnp.einsum('oi,to->it', basis_out, masked, preferred_element_type=jnp.flo...  13.9 us
  transfers between devices with their start and end apart: 4, of which 4 were waited for; matrix products, arithmetic and copies ran while one was open for 4% of the time, Pallas kernels for 0%

commit v1 on v0

v1 whole, which is shorter than its diff:
```python
import jax
import jax.numpy as jnp
from jax import lax
from jax.experimental import pallas as pl
from jax.experimental.pallas import tpu as pltpu
from jax.sharding import PartitionSpec as P

LEN = 256
MESH = pl.DeviceIdType.MESH
F32, BF16 = jnp.float32, jnp.bfloat16
ORDER = (4, 3, -3, 2, -2, 1, -1, 0)
GROUPS = ((0, 1), (1, 3), (3, 5), (5, 7), (7, 8))
QS = 4


def kernel(
    acts, grads, bout, bin_, slot_seq, seq_len, out,
    g, bo, bp, a, bi, ra, sb, rb, sq, cr, ts, tr,
    loc, g_s, g_r, py_s, py_r, px_s, px_r, pc_s, pc_r,
    az_s, az_r, ay_s, ay_r, bz_s, bz_r, by_s, by_r, bl_s, bl_r,
    bx_s, bx_r, bc_s, bc_r, rs_s, rs_r, cs_s, cs_r, ts_s, ts_r,
):
    d, t = lax.axis_index("dp"), lax.axis_index("tensor")
    yl, x, c = d // 8, (d // 2) % 4, d % 2
    z, yh = t // 2, t % 2

    def dev(dx=0, dz=0, flip_yl=False, flip_c=False, flip_yh=False):
        nyl = 1 - yl if flip_yl else yl
        nc = 1 - c if flip_c else c
        nyh = 1 - yh if flip_yh else yh
        return (nyl * 8 + (x + dx + 4) % 4 * 2 + nc, (z + dz + 8) % 8 * 2 + nyh)

    def remote(src, dst, s, r, to):
        return pltpu.make_async_remote_copy(
            src_ref=src, dst_ref=dst, send_sem=s, recv_sem=r,
            device_id=to, device_id_type=MESH,
        )

    pending = []

    def send(src, dst, s, r, to):
        copy = remote(src, dst, s, r, to)
        copy.start()
        pending.append(copy)

    def arrived(dst, s, r):
        remote(dst, dst, s, r, dev(dz=1)).wait_recv()

    def way(i):
        return 1 - 2 * i

    partners = [dev(dz=1), dev(dz=-1), dev(flip_yh=True), dev(flip_yl=True, flip_yh=True), dev(flip_c=True)]
    partners += [dev(dx=j, flip_yl=u == 1) for u in range(2) for j in range(4) if u or j]
    barrier = pltpu.get_barrier_semaphore()
    for to in partners:
        pl.semaphore_signal(barrier, inc=1, device_id=to, device_id_type=MESH)

    def column(k, h):
        return pl.multiple_of(((z + ORDER[k] + 8) % 8 * 2 + h) * 512, 512)

    blk = yl * 4 + x
    my_cols = pl.multiple_of(d * 128, 128)
    local = [
        pltpu.make_async_copy(acts, a.at[yh, z], loc.at[8]),
        pltpu.make_async_copy(bin_.at[:, pl.ds(my_cols, 128)], bi.at[blk, c, yh, z], loc.at[9]),
        pltpu.make_async_copy(grads, g.at[0], loc.at[10]),
    ]
    local += [pltpu.make_async_copy(bout.at[:, pl.ds(column(k, yh), 512)], bo.at[k], loc.at[k]) for k in range(8)]
    for copy in local:
        copy.start()
    pl.semaphore_wait(barrier, len(partners))

    def bz(i, h):
        ref = bi.at[blk, c, yh, (z - way(i) * h + 8) % 8]
        return ref.at[pl.ds(64 * i, 64)] if h == 4 else ref

    def az(i, h):
        ref = a.at[yh, (z - way(i) * h + 8) % 8]
        return ref.at[pl.ds(256 * i, 256)] if h == 4 else ref

    def half(ref, i, rows, h):
        return ref.at[pl.ds(rows * i, rows)] if h == 4 else ref

    def hop(h):
        for i in range(2):
            to = dev(dz=way(i))
            origin = (z - way(i) * (h - 1) + 8) % 8
            src = bi.at[blk, c, yh, origin] if h > 1 else bin_.at[:, pl.ds(my_cols, 128)]
            send(half(src, i, 64, h), half(bi.at[blk, c, yh, origin], i, 64, h), bz_s.at[i, h - 1], bz_r.at[i, h - 1], to)
        for i in range(2):
            to = dev(dz=way(i))
            origin = (z - way(i) * (h - 1) + 8) % 8
            src = a.at[yh, origin] if h > 1 else acts
            send(half(src, i, 256, h), half(a.at[yh, origin], i, 256, h), az_s.at[i, h - 1], az_r.at[i, h - 1], to)

    def hop_arrived(h):
        for i in range(2):
            arrived(bz(i, h), bz_s.at[i, h - 1], bz_r.at[i, h - 1])
        for i in range(2):
            arrived(az(i, h), az_s.at[i, h - 1], az_r.at[i, h - 1])

    def rows(dx):
        return pl.multiple_of(c * 256 + (x + dx + 4) % 4 * 64, 64)

    def p_first(k):
        row, cut = rows(0), pl.ds(column(k, 1 - yh), 512)
        to = dev(flip_yl=True, flip_yh=True)
        send(bout.at[pl.ds(row, 64), cut], bp.at[k, pl.ds(row, 64)], py_s.at[k], py_r.at[k], to)

    def p_x(n):
        lo, hi = GROUPS[n]
        for k in range(lo, hi):
            arrived(bp.at[k, pl.ds(rows(0), 64)], py_s.at[k], py_r.at[k])
        ref = bp.at[pl.ds(lo, hi - lo), pl.ds(rows(0), 64)]
        for i in range(2):
            send(ref, ref, px_s.at[n, i], px_r.at[n, i], dev(dx=way(i)))

    def p_relay(n):
        lo, hi = GROUPS[n]
        for i in range(2):
            row = rows(-way(i))
            arrived(bp.at[pl.ds(lo, hi - lo), pl.ds(row, 64)], px_s.at[n, i], px_r.at[n, i])
            ref = bp.at[pl.ds(lo, hi - lo), pl.ds(row + 32 * i, 32)]
            send(ref, ref, px_s.at[n, 2 + i], px_r.at[n, 2 + i], dev(dx=way(i)))

    def p_core(n):
        lo, hi = GROUPS[n]
        for i in range(2):
            ref = bp.at[pl.ds(lo, hi - lo), pl.ds(rows(2) + 32 * i, 32)]
            arrived(ref, px_s.at[n, 2 + i], px_r.at[n, 2 + i])
        ref = bp.at[pl.ds(lo, hi - lo), pl.ds(pl.multiple_of(c * 256, 256), 256)]
        send(ref, ref, pc_s.at[n], pc_r.at[n], dev(flip_c=True))

    def p_ready(n):
        lo, hi = GROUPS[n]
        ref = bp.at[pl.ds(lo, hi - lo), pl.ds(pl.multiple_of((1 - c) * 256, 256), 256)]
        arrived(ref, pc_s.at[n], pc_r.at[n])

    def b_of(u, dx):
        return (1 - yl if u else yl) * 4 + (x + dx + 4) % 4

    def b_start(u):
        ref = bi.at[b_of(u, 0), c]
        for i in range(2):
            send(ref, ref, bx_s.at[u, i], bx_r.at[u, i], dev(dx=way(i)))
        send(ref, ref, bc_s.at[u, 0], bc_r.at[u, 0], dev(flip_c=True))

    def b_relay(u):
        for i in range(2):
            ref = bi.at[b_of(u, -way(i)), c]
            arrived(ref, bx_s.at[u, i], bx_r.at[u, i])
            part = bi.at[b_of(u, -way(i)), c, i]
            send(part, part, bx_s.at[u, 2 + i], bx_r.at[u, 2 + i], dev(dx=way(i)))
            send(ref, ref, bc_s.at[u, 1 + i], bc_r.at[u, 1 + i], dev(flip_c=True))

    def b_last(u):
        for i in range(2):
            arrived(bi.at[b_of(u, 2), c, i], bx_s.at[u, 2 + i], bx_r.at[u, 2 + i])
        ref = bi.at[b_of(u, 2), c]
        send(ref, ref, bc_s.at[u, 3], bc_r.at[u, 3], dev(flip_c=True))

    def rotate(u, n):
        b = b_of(u, (0, -1, 1, 2)[n])
        arrived(bi.at[b, 1 - c], bc_s.at[u, n], bc_r.at[u, n])

        def tile(i, carry):
            row = pl.multiple_of(i * 128, 128)
            left = jnp.concatenate([a[k // 8, k % 8, pl.ds(row, 128), :] for k in range(16)], axis=1)
            right = jnp.concatenate([bi[b, e].reshape(2048, 128) for e in range(2)], axis=1)
            count = seq_len[slot_seq[d * 2 + i // 2]]
            place = lax.broadcasted_iota(jnp.int32, (128, 256), 0) + (i % 2) * 128
            rot = jnp.dot(left, right, preferred_element_type=F32)
            ra[b, pl.ds(row, 128), :] = jnp.where(place < count, rot, 0.0).astype(BF16)
            return carry

        lax.fori_loop(0, 4, tile, 0)

    def product(k, q, lo=0, n=512):
        cut = pl.ds(pl.multiple_of(q * 128, 128), 128)
        own = jnp.dot(g[0, pl.ds(lo, n), :], bo[k, :, cut], preferred_element_type=F32)
        return own + jnp.dot(g[1, pl.ds(lo, n), :], bp[k, :, cut], preferred_element_type=F32)

    def part(ref, i, s, q):
        return ref.at[0, s, q, pl.ds(256 * i, 256)] if s == 0 else ref.at[i, s, q]

    def rs_copy(i, s, q):
        return remote(part(sb, i, s, q), part(rb, i, s, q), rs_s.at[i, s, q], rs_r.at[i, s, q], dev(dz=way(i)))

    def rs_arrived(i, s, q):
        arrived(part(rb, i, s, q), rs_s.at[i, s, q], rs_r.at[i, s, q])

    def stage(s, q):
        if s == 0:
            sb[0, 0, q] = product(0, q).astype(BF16)
            for i in range(2):
                rs_copy(i, 0, q).start()
            return
        for i in range(2):
            rs_arrived(i, s - 1, q)
            k = 2 * s - 1 + i
            if s == 1:
                lo, no = 256 * i, 256 * (1 - i)
                with_sum = product(k, q, lo, 256) + rb[0, 0, q, pl.ds(lo, 256), :].astype(F32)
                sb[i, s, q, pl.ds(lo, 256), :] = with_sum.astype(BF16)
                sb[i, s, q, pl.ds(no, 256), :] = product(k, q, no, 256).astype(BF16)
            else:
                sb[i, s, q] = (product(k, q) + rb[i, s - 1, q].astype(F32)).astype(BF16)
            rs_copy(i, s, q).start()

    def stages(s):
        def body(q, carry):
            stage(s, q)
            return carry

        lax.fori_loop(0, QS, body, 0)

    def squares(q):
        for i in range(2):
            rs_arrived(i, 3, q)
        rot = product(7, q) + rb[0, 3, q].astype(F32) + rb[1, 3, q].astype(F32)
        rot = rot.T.astype(BF16)

        def body(b, carry):
            total = None
            for slot in range(2):
                span = slice(slot * LEN, (slot + 1) * LEN)
                r = jnp.dot(rot[:, span], ra[b, span, :], preferred_element_type=F32)
                total = r * r if total is None else total + r * r
            sq[q, 0, b] = total[:, :128]
            sq[q, 1, b] = total[:, 128:]
            return carry

        lax.fori_loop(0, 8, body, 0)
        send(sq.at[q, 1 - c], cr.at[q], cs_s.at[q], cs_r.at[q], dev(flip_c=True))

    others = [(u, j) for u in range(2) for j in range(4) if u or j]

    def spread(q):
        arrived(cr.at[q], cs_s.at[q], cs_r.at[q])

        def body(b, carry):
            ts[q, b] = (sq[q, c, b] + cr[q, b]).astype(BF16)
            return carry

        lax.fori_loop(0, 8, body, 0)
        for u, j in others:
            send(ts.at[q, b_of(u, j)], tr.at[q, blk], ts_s.at[q, u, j], ts_r.at[q, u, j], dev(dx=j, flip_yl=u == 1))

    def finish(q):
        total = sq[q, c, blk] + cr[q, blk]
        for u, j in others:
            b = b_of(u, -j)
            arrived(tr.at[q, b], ts_s.at[q, u, j], ts_r.at[q, u, j])
            total = total + tr[q, b].astype(F32)
        out[pl.ds(q * 128, 128), :] = total * (1.0 / (32 * LEN))

    hop(1)
    send(grads, g.at[1], g_s, g_r, dev(flip_yh=True))
    for k in range(8):
        p_first(k)
    for h in range(1, 5):
        hop_arrived(h)
        if h == 1:
            local[0].wait()
            local[1].wait()
        if h < 4:
            hop(h + 1)
        p_x(h - 1)
        if h > 1:
            p_relay(h - 2)
        if h > 2:
            p_core(h - 3)
    ref = bi.at[blk, c, yh]
    send(ref, ref, by_s, by_r, dev(flip_yh=True))
    for copy in local[2:]:
        copy.wait()
    arrived(g.at[1], g_s, g_r)
    p_ready(0)
    send(a.at[yh], a.at[yh], ay_s, ay_r, dev(flip_yh=True))
    stages(0)
    p_x(4)
    p_relay(3)
    p_core(2)
    arrived(bi.at[blk, c, 1 - yh], by_s, by_r)
    ref = bi.at[blk, c]
    send(ref, ref, bl_s, bl_r, dev(flip_yl=True))
    b_start(0)
    p_ready(1)
    stages(1)
    p_relay(4)
    p_core(3)
    p_core(4)
    b_relay(0)
    arrived(bi.at[b_of(1, 0), c], bl_s, bl_r)
    b_start(1)
    p_ready(2)
    stages(2)
    b_last(0)
    b_relay(1)
    p_ready(3)
    p_ready(4)
    stages(3)
    arrived(a.at[1 - yh], ay_s, ay_r)
    for n in range(4):
        rotate(0, n)
    b_last(1)
    for n in range(4):
        rotate(1, n)
    for q in range(QS + 2):
        if q < QS:
            squares(q)
        if 1 <= q <= QS:
            spread(q - 1)
        if q >= 2:
            finish(q - 2)

    for copy in pending:
        copy.wait_send()
    for s in range(4):
        for i in range(2):

            def left(q, carry, i=i, s=s):
                rs_copy(i, s, q).wait_send()
                return carry

            lax.fori_loop(0, QS, left, 0)


def shards(acts, out_grads, basis_out, basis_in, slot_sequence, seq_lengths):
    sem = pltpu.SemaphoreType.DMA
    any_, smem = pl.BlockSpec(memory_space=pl.ANY), pl.BlockSpec(memory_space=pltpu.SMEM)
    pair = lambda *shape: [sem(shape)] * 2
    return pl.pallas_call(
        kernel,
        name="eigenvalues",
        out_shape=jax.ShapeDtypeStruct((512, 128), F32),
        in_specs=[any_] * 4 + [smem] * 2,
        out_specs=pl.BlockSpec(memory_space=pltpu.VMEM),
        scratch_shapes=[
            pltpu.VMEM((2, 512, 512), BF16),
            pltpu.VMEM((8, 512, 512), BF16),
            pltpu.VMEM((8, 512, 512), BF16),
            pltpu.VMEM((2, 8, 512, 128), BF16),
            pltpu.VMEM((8, 2, 2, 8, 128, 128), BF16),
            pltpu.VMEM((8, 512, 256), BF16),
            pltpu.VMEM((2, 4, QS, 512, 128), BF16),
            pltpu.VMEM((2, 4, QS, 512, 128), BF16),
            pltpu.VMEM((QS, 2, 8, 128, 128), F32),
            pltpu.VMEM((QS, 8, 128, 128), F32),
            pltpu.VMEM((QS, 8, 128, 128), BF16),
            pltpu.VMEM((QS, 8, 128, 128), BF16),
            sem((11,)),
            *[sem, sem],
            *pair(8), *pair(5, 4), *pair(5),
            *pair(2, 4), *[sem, sem], *pair(2, 4), *[sem, sem], *[sem, sem],
            *pair(2, 4), *pair(2, 4), *pair(2, 4, QS), *pair(QS), *pair(QS, 2, 4),
        ],
        compiler_params=pltpu.CompilerParams(
            collective_id=0, has_side_effects=True, vmem_limit_bytes=56 << 20
        ),
        cost_estimate=pl.CostEstimate(flops=10 * 2**30, bytes_accessed=12 << 20, transcendentals=0),
    )(acts, out_grads, basis_out, basis_in, slot_sequence, seq_lengths)


def solution(mesh):
    return jax.shard_map(
        shards,
        mesh=mesh,
        in_specs=(
            P("dp", "tensor"),
            P("dp", "tensor"),
            P("tensor", None),
            P("tensor", None),
            P(),
            P(),
        ),
        out_specs=P("tensor", "dp"),
        check_vma=False,
    )
```

time: 603 us -> 130 us (0.22)
  waiting for transfers between devices: 557 us -> 0 us
  Pallas kernels: 0 us -> 128 us
  matrix products: 25.8 us -> 0 us
  between operations: 13.2 us -> 0.01 us
    reduce_scatter x2 -> x0, waiting for transfers between devices: 346 us -> none  [the longest x1 282 us: shards(): lax.psum_scatter(jnp.einsum('oi,to->it', basis_out, masked, preferred_ele...]
    all_gather x2 -> x0, waiting for transfers between devices: 210 us -> none  [the longest x1 138 us: shards(): lax.all_gather(basis_in, 'tensor', axis=0, tiled=True)]
    pallas_call x0 -> x1, Pallas kernels: none -> 128 us  [shards(): pl.pallas_call(kernel, name='eigenvalues', out_shape=jax.ShapeDtypeStruct...]
    dot_general x4 -> x0, matrix products: 25.8 us -> none  [the longest x1 13.9 us: shards(): jnp.einsum('oi,to->it', basis_out, masked, preferred_element_type=jnp.flo...]
  transfers between devices with their start and end apart: 4 -> 0, of which waited for: 4 -> 0; matrix products, arithmetic and copies ran while one was open for 4% -> 0% of each run, Pallas kernels for 0% -> 0%
where the time goes in v1:
time: 130 us
  Pallas kernels  128 us (98%)
  local copies, waits for them, and re-layouts  1.67 us (1%)
    pallas_call x1, Pallas kernels, shards(): pl.pallas_call(kernel, name='eigenvalues', out_shape=jax.ShapeDtypeStruct...  128 us

profile of v1, /device:TPU:1, one launch (start us, length us, event | category | flops | bytes accessed | tf_op | source)
XLA Modules:
  0.0 129.9 jit_solution(4103337603745662794)
XLA Ops:
  0.0 128.2 %eigenvalues.1 = f32[512,128]{1,0:T(8,128)} custom-call(bf16[512,128]{1,0:T(8,128)(2,1)} %acts.1, bf16[512,512]{1,0:T(8,128)(2,1)} %grads.1, bf16[512,8192]{1,0:T(8,128)(2,1)} %bout.1, bf16[128,2048]{1,0:T(8,128)(2,1)} %bin_.1, s32[32]{0:T(128)} %slot_seq.1, s32[32]{0:T(128)} %seq_len.1), custom_call_target="tpu_custom_call" | custom-call | flops 10737418240 | bytes 12582912 | tf_op jit(solution)/shard_map/eigenvalues/pallas_call | solution.py:333
  128.2 1.7 %copy.8 = f32[512,128]{1,0:T(8,128)} copy(f32[512,128]{1,0:T(8,128)} %eigenvalues.1) | data formatting | bytes 524288

commit v2 on v0

v2 whole, which is shorter than its diff:
```python
import jax
import jax.numpy as jnp
from jax import lax
from jax.experimental import pallas as pl
from jax.experimental.pallas import tpu as pltpu
from jax.sharding import PartitionSpec as P

LEN = 256
MESH = pl.DeviceIdType.MESH
F32, BF16 = jnp.float32, jnp.bfloat16
ORDER = (4, 3, -3, 2, -2, 1, -1, 0)
GROUPS = ((0, 1), (1, 3), (3, 5), (5, 7), (7, 8))
QS = 4
WORK = (
    ("bhop", 1), ("py", 0), ("ahop", 1), ("py", 1), ("bw", 1), ("py", 2), ("bhop", 2), ("aw", 1), ("g",),
    ("px", 0), ("bw", 2), ("bhop", 3), ("ahop", 2), ("py", 4), ("px", 1), ("px", 2), ("bw", 3), ("pr", 0),
    ("bhop", 4), ("aw", 2), ("px", 4), ("pr", 1), ("pc", 0), ("bw", 4), ("ahop", 3), ("bs", 0, 0), ("pc", 1),
    ("bs", 0, 1), ("by", 0), ("aw", 3), ("pw", 0), ("gw",), ("pr", 2), ("py", 3), ("st", 0, 0), ("ahop", 4),
    ("pc", 2), ("st", 0, 1), ("by", 1), ("pw", 1), ("aw", 4), ("px", 3), ("st", 1, 0), ("ay", 1), ("byw", 0),
    ("rotA", 0), ("bs", 1, 0), ("pr", 4), ("br", 0, 0), ("st", 1, 1), ("br", 0, 1), ("pr", 3), ("pw", 2),
    ("st", 2, 0), ("byw", 1), ("ay", 0), ("rotA", 1), ("pc", 4), ("bs", 1, 1), ("pc", 3), ("st", 2, 1),
    ("pw", 3), ("ayw", 1), ("pw", 4), ("br", 1, 0), ("bl", 0, 1), ("st", 3, 0), ("bl", 0, 0), ("rotA", 2),
    ("br", 1, 1), ("rotA", 3), ("own",), ("bl", 1, 0), ("st", 3, 1), ("ayw", 0), ("rotB", 2), ("bl", 1, 1),
    ("rotB", 0), ("rotB", 3), ("rotB", 1), ("sq", 1), ("sq", 0), ("spr", 1), ("spr", 0), ("sq", 3),
    ("spr", 3), ("sq", 2), ("fin", 1), ("spr", 2), ("fin", 3), ("fin", 0), ("fin", 2),
)


def kernel(
    acts, grads, bout, bin_, slot_seq, seq_len, out,
    g, bo, bp, a, bi, ra, acc, sb, rb, ownp, sq, cr, ts, tr,
    loc, g_s, g_r, py_s, py_r, px_s, px_r, pc_s, pc_r,
    az_s, az_r, ay_s, ay_r, bz_s, bz_r, by_s, by_r,
    bx_s, bx_r, bc_s, bc_r, rs_s, rs_r, cs_s, cs_r, ts_s, ts_r,
):
    d, t = lax.axis_index("dp"), lax.axis_index("tensor")
    yl, x, c = d // 8, (d // 2) % 4, d % 2
    z, yh = t // 2, t % 2

    def dev(dx=0, dz=0, flip_yl=False, flip_c=False, flip_yh=False):
        nyl = 1 - yl if flip_yl else yl
        nc = 1 - c if flip_c else c
        nyh = 1 - yh if flip_yh else yh
        return (nyl * 8 + (x + dx + 4) % 4 * 2 + nc, (z + dz + 8) % 8 * 2 + nyh)

    def remote(src, dst, s, r, to):
        return pltpu.make_async_remote_copy(
            src_ref=src, dst_ref=dst, send_sem=s, recv_sem=r,
            device_id=to, device_id_type=MESH,
        )

    pending = []

    def send(src, dst, s, r, to):
        copy = remote(src, dst, s, r, to)
        copy.start()
        pending.append(copy)

    def arrived(dst, s, r):
        remote(dst, dst, s, r, dev(dz=1)).wait_recv()

    def way(i):
        return 1 - 2 * i

    neighbour = dev(flip_yl=True, flip_yh=True)
    partners = [dev(dz=1), dev(dz=-1), dev(flip_yh=True), neighbour, dev(flip_c=True)]
    others = [(u, j) for u in range(2) for j in range(4) if u or j]
    partners += [dev(dx=j, flip_yl=u == 1) for u, j in others]
    barrier = pltpu.get_barrier_semaphore()
    for to in partners:
        pl.semaphore_signal(barrier, inc=1, device_id=to, device_id_type=MESH)

    def column(k, h):
        return pl.multiple_of(((z + ORDER[k] + 8) % 8 * 2 + h) * 512, 512)

    me = x * 2 + c
    my_cols = pl.multiple_of(me * 256, 256)
    local = [
        pltpu.make_async_copy(acts, a.at[yh, z], loc.at[8]),
        pltpu.make_async_copy(bin_.at[:, pl.ds(my_cols, 256)], bi.at[me, yh, z], loc.at[9]),
        pltpu.make_async_copy(grads, g.at[0], loc.at[10]),
    ]
    local += [pltpu.make_async_copy(bout.at[:, pl.ds(column(k, yh), 512)], bo.at[k], loc.at[k]) for k in range(8)]
    for copy in local:
        copy.start()
    pl.semaphore_wait(barrier, len(partners))

    def half(ref, i, rows, h):
        return ref.at[pl.ds(rows * i, rows)] if h == 4 else ref

    def bhop(h):
        for i in range(2):
            origin = (z - way(i) * (h - 1) + 8) % 8
            src = bi.at[me, yh, origin] if h > 1 else bin_.at[:, pl.ds(my_cols, 256)]
            send(half(src, i, 64, h), half(bi.at[me, yh, origin], i, 64, h), bz_s.at[i, h - 1], bz_r.at[i, h - 1], dev(dz=way(i)))

    def bw(h):
        for i in range(2):
            ref = half(bi.at[me, yh, (z - way(i) * h + 8) % 8], i, 64, h)
            arrived(ref, bz_s.at[i, h - 1], bz_r.at[i, h - 1])
        if h == 4:
            local[1].wait()

    def ahop(h):
        for i in range(2):
            origin = (z - way(i) * (h - 1) + 8) % 8
            src = a.at[yh, origin] if h > 1 else acts
            send(half(src, i, 256, h), half(a.at[yh, origin], i, 256, h), az_s.at[i, h - 1], az_r.at[i, h - 1], dev(dz=way(i)))

    def aw(h):
        for i in range(2):
            ref = half(a.at[yh, (z - way(i) * h + 8) % 8], i, 256, h)
            arrived(ref, az_s.at[i, h - 1], az_r.at[i, h - 1])
        if h == 4:
            local[0].wait()

    def by(v):
        ref = bi.at[me, yh, pl.ds(4 * v, 4)]
        send(ref, ref, by_s.at[v], by_r.at[v], neighbour)

    def byw(v):
        arrived(bi.at[me, 1 - yh, pl.ds(4 * v, 4)], by_s.at[v], by_r.at[v])

    def ay(v):
        ref = a.at[yh, pl.ds(4 * v, 4)]
        send(ref, ref, ay_s.at[v], ay_r.at[v], dev(flip_yh=True))

    def ayw(v):
        arrived(a.at[1 - yh, pl.ds(4 * v, 4)], ay_s.at[v], ay_r.at[v])

    def gsend():
        send(grads, g.at[1], g_s, g_r, dev(flip_yh=True))

    def gw():
        arrived(g.at[1], g_s, g_r)
        for copy in local[2:]:
            copy.wait()

    def rows(dx):
        return pl.multiple_of(c * 256 + (x + dx + 4) % 4 * 64, 64)

    def span(n):
        return pl.ds(GROUPS[n][0], GROUPS[n][1] - GROUPS[n][0])

    def py(n):
        for k in range(*GROUPS[n]):
            row, cut = rows(0), pl.ds(column(k, 1 - yh), 512)
            send(bout.at[pl.ds(row, 64), cut], bp.at[k, pl.ds(row, 64)], py_s.at[k], py_r.at[k], neighbour)

    def px(n):
        for k in range(*GROUPS[n]):
            arrived(bp.at[k, pl.ds(rows(0), 64)], py_s.at[k], py_r.at[k])
        ref = bp.at[span(n), pl.ds(rows(0), 64)]
        for i in range(2):
            send(ref, ref, px_s.at[n, i], px_r.at[n, i], dev(dx=way(i)))

    def pr(n):
        for i in range(2):
            row = rows(-way(i))
            arrived(bp.at[span(n), pl.ds(row, 64)], px_s.at[n, i], px_r.at[n, i])
            ref = bp.at[span(n), pl.ds(row + 32 * i, 32)]
            send(ref, ref, px_s.at[n, 2 + i], px_r.at[n, 2 + i], dev(dx=way(i)))

    def pc(n):
        for i in range(2):
            arrived(bp.at[span(n), pl.ds(rows(2) + 32 * i, 32)], px_s.at[n, 2 + i], px_r.at[n, 2 + i])
        ref = bp.at[span(n), pl.ds(pl.multiple_of(c * 256, 256), 256)]
        send(ref, ref, pc_s.at[n], pc_r.at[n], dev(flip_c=True))

    def pw(n):
        arrived(bp.at[span(n), pl.ds(pl.multiple_of((1 - c) * 256, 256), 256)], pc_s.at[n], pc_r.at[n])

    def block(dx, e):
        return (x + dx + 4) % 4 * 2 + e

    def b_part(dx, e, u, v):
        return bi.at[block(dx, e), 1 - yh if u else yh, pl.ds(4 * v, 4)]

    def to_core(dx, u, v, n):
        ref = b_part(dx, c, u, v)
        send(ref, ref, bc_s.at[u, v, n], bc_r.at[u, v, n], dev(flip_c=True))

    def bs(u, v):
        ref = b_part(0, c, u, v)
        for i in range(2):
            send(ref, ref, bx_s.at[u, v, i], bx_r.at[u, v, i], dev(dx=way(i)))
        to_core(0, u, v, 0)

    def br(u, v):
        for i in range(2):
            ref = b_part(-way(i), c, u, v)
            arrived(ref, bx_s.at[u, v, i], bx_r.at[u, v, i])
            part = ref.at[pl.ds(2 * i, 2)]
            send(part, part, bx_s.at[u, v, 2 + i], bx_r.at[u, v, 2 + i], dev(dx=way(i)))
            to_core(-way(i), u, v, 1 + i)

    def bl(u, v):
        for i in range(2):
            arrived(b_part(2, c, u, v).at[pl.ds(2 * i, 2)], bx_s.at[u, v, 2 + i], bx_r.at[u, v, 2 + i])
        to_core(2, u, v, 3)

    def rot_half(b, h):
        left = jnp.concatenate([a[h, k] for k in range(8)], axis=1)
        return jnp.dot(left, bi[b, h].reshape(1024, 256), preferred_element_type=F32)

    def rot(n, u):
        dx = (0, -1, 1, 2)[n]
        for e in (c, 1 - c):
            b = block(dx, e)
            if e is not c:
                for v in range(2):
                    arrived(b_part(dx, e, u, v), bc_s.at[u, v, n], bc_r.at[u, v, n])
            if u == 0:
                acc[b] = rot_half(b, yh)
            else:
                total = acc[b] + rot_half(b, 1 - yh)
                place = lax.broadcasted_iota(jnp.int32, (LEN, 256), 0)
                for slot in range(2):
                    count = seq_len[slot_seq[d * 2 + slot]]
                    part = total[slot * LEN : (slot + 1) * LEN]
                    ra[b, pl.ds(slot * LEN, LEN), :] = jnp.where(place < count, part, 0.0).astype(BF16)

    def product(k, pair):
        cut = pl.ds(pair * 256, 256)
        own = jnp.dot(g[0], bo[k, :, cut], preferred_element_type=F32)
        return own + jnp.dot(g[1], bp[k, :, cut], preferred_element_type=F32)

    def rs_part(ref, i, s, q):
        return ref.at[0, s, q, pl.ds(256 * i, 256)] if s == 0 else ref.at[i, s, q]

    def rs_send(i, s, q):
        send(rs_part(sb, i, s, q), rs_part(rb, i, s, q), rs_s.at[i, s, q], rs_r.at[i, s, q], dev(dz=way(i)))

    def rs_arrived(i, s, q):
        arrived(rs_part(rb, i, s, q), rs_s.at[i, s, q], rs_r.at[i, s, q])

    def st(s, pair):
        if s == 0:
            total = product(0, pair)
            for e in range(2):
                sb[0, 0, 2 * pair + e] = total[:, e * 128 : (e + 1) * 128].astype(BF16)
            for i in range(2):
                for e in range(2):
                    rs_send(i, 0, 2 * pair + e)
            return
        for i in range(2):
            total = product(2 * s - 1 + i, pair)
            for e in range(2):
                q, mine = 2 * pair + e, total[:, e * 128 : (e + 1) * 128]
                rs_arrived(i, s - 1, q)
                if s == 1:
                    lo, no = 256 * i, 256 * (1 - i)
                    with_sum = mine[lo : lo + 256] + rb[0, 0, q, pl.ds(lo, 256), :].astype(F32)
                    sb[i, s, q, pl.ds(lo, 256), :] = with_sum.astype(BF16)
                    sb[i, s, q, pl.ds(no, 256), :] = mine[no : no + 256].astype(BF16)
                else:
                    sb[i, s, q] = (mine + rb[i, s - 1, q].astype(F32)).astype(BF16)
                rs_send(i, s, q)

    def own():
        for pair in range(2):
            ownp[:, pl.ds(pair * 256, 256)] = product(7, pair)

    blk = yl * 4 + x

    def squares(q):
        for i in range(2):
            rs_arrived(i, 3, q)
        rotated = ownp[:, pl.ds(q * 128, 128)] + rb[0, 3, q].astype(F32) + rb[1, 3, q].astype(F32)
        rotated = rotated.T.astype(BF16)
        for b in range(8):
            total = None
            for slot in range(2):
                rng = slice(slot * LEN, (slot + 1) * LEN)
                r = jnp.dot(rotated[:, rng], ra[b, rng, :], preferred_element_type=F32)
                total = r * r if total is None else total + r * r
            sq[q, 0, b] = total[:, :128]
            sq[q, 1, b] = total[:, 128:]
        send(sq.at[q, 1 - c], cr.at[q], cs_s.at[q], cs_r.at[q], dev(flip_c=True))

    def chip(u, j):
        return (1 - yl if u else yl) * 4 + (x + j + 4) % 4

    def spread(q):
        arrived(cr.at[q], cs_s.at[q], cs_r.at[q])
        for u, j in others:
            b = chip(u, j)
            ts[q, b] = (sq[q, c, b] + cr[q, b]).astype(BF16)
            send(ts.at[q, b], tr.at[q, blk], ts_s.at[q, u, j], ts_r.at[q, u, j], dev(dx=j, flip_yl=u == 1))

    def finish(q):
        total = sq[q, c, blk] + cr[q, blk]
        for u, j in others:
            b = chip(u, -j)
            arrived(tr.at[q, b], ts_s.at[q, u, j], ts_r.at[q, u, j])
            total = total + tr[q, b].astype(F32)
        out[pl.ds(q * 128, 128), :] = total * (1.0 / (32 * LEN))

    steps = dict(
        bhop=bhop, bw=bw, ahop=ahop, aw=aw, by=by, byw=byw, ay=ay, ayw=ayw, g=gsend, gw=gw,
        py=py, px=px, pr=pr, pc=pc, pw=pw, bs=bs, br=br, bl=bl,
        rotA=lambda n: rot(n, 0), rotB=lambda n: rot(n, 1), st=st, own=own,
        sq=squares, spr=spread, fin=finish,
    )
    for name, *what in WORK:
        steps[name](*what)
    for copy in pending:
        copy.wait_send()


def shards(acts, out_grads, basis_out, basis_in, slot_sequence, seq_lengths):
    sem = pltpu.SemaphoreType.DMA
    any_, smem = pl.BlockSpec(memory_space=pl.ANY), pl.BlockSpec(memory_space=pltpu.SMEM)
    pair = lambda *shape: [sem(shape)] * 2
    return pl.pallas_call(
        kernel,
        name="eigenvalues",
        out_shape=jax.ShapeDtypeStruct((512, 128), F32),
        in_specs=[any_] * 4 + [smem] * 2,
        out_specs=pl.BlockSpec(memory_space=pltpu.VMEM),
        scratch_shapes=[
            pltpu.VMEM((2, 512, 512), BF16),
            pltpu.VMEM((8, 512, 512), BF16),
            pltpu.VMEM((8, 512, 512), BF16),
            pltpu.VMEM((2, 8, 512, 128), BF16),
            pltpu.VMEM((8, 2, 8, 128, 256), BF16),
            pltpu.VMEM((8, 512, 256), BF16),
            pltpu.VMEM((8, 512, 256), F32),
            pltpu.VMEM((2, 4, QS, 512, 128), BF16),
            pltpu.VMEM((2, 4, QS, 512, 128), BF16),
            pltpu.VMEM((512, 512), F32),
            pltpu.VMEM((QS, 2, 8, 128, 128), F32),
            pltpu.VMEM((QS, 8, 128, 128), F32),
            pltpu.VMEM((QS, 8, 128, 128), BF16),
            pltpu.VMEM((QS, 8, 128, 128), BF16),
            sem((11,)),
            *[sem, sem],
            *pair(8), *pair(5, 4), *pair(5),
            *pair(2, 4), *pair(2), *pair(2, 4), *pair(2),
            *pair(2, 2, 4), *pair(2, 2, 4), *pair(2, 4, QS), *pair(QS), *pair(QS, 2, 4),
        ],
        compiler_params=pltpu.CompilerParams(
            collective_id=0, has_side_effects=True, vmem_limit_bytes=56 << 20
        ),
        cost_estimate=pl.CostEstimate(flops=10 * 2**30, bytes_accessed=12 << 20, transcendentals=0),
    )(acts, out_grads, basis_out, basis_in, slot_sequence, seq_lengths)


def solution(mesh):
    return jax.shard_map(
        shards,
        mesh=mesh,
        in_specs=(
            P("dp", "tensor"),
            P("dp", "tensor"),
            P("tensor", None),
            P("tensor", None),
            P(),
            P(),
        ),
        out_specs=P("tensor", "dp"),
        check_vma=False,
    )
```

time: 603 us -> 120 us (0.20)
  the two profiles are of different devices: /device:TPU:1 before, /device:TPU:16 now
where the time goes in v2:
time: 120 us
  Pallas kernels  118 us (98%)
  local copies, waits for them, and re-layouts  1.67 us (1%)
    pallas_call x1, Pallas kernels, shards(): pl.pallas_call(kernel, name='eigenvalues', out_shape=jax.ShapeDtypeStruct...  118 us

profile of v2, /device:TPU:16, one launch (start us, length us, event | category | flops | bytes accessed | tf_op | source)
XLA Modules:
  0.0 119.8 jit_solution(3904048658326875877)
XLA Ops:
  0.0 118.1 %eigenvalues.1 = f32[512,128]{1,0:T(8,128)} custom-call(bf16[512,128]{1,0:T(8,128)(2,1)} %acts.1, bf16[512,512]{1,0:T(8,128)(2,1)} %grads.1, bf16[512,8192]{1,0:T(8,128)(2,1)} %bout.1, bf16[128,2048]{1,0:T(8,128)(2,1)} %bin_.1, s32[32]{0:T(128)} %slot_seq.1, s32[32]{0:T(128)} %seq_len.1), custom_call_target="tpu_custom_call" | custom-call | flops 10737418240 | bytes 12582912 | tf_op jit(solution)/shard_map/eigenvalues/pallas_call | solution.py:315
  118.1 1.7 %copy.8 = f32[512,128]{1,0:T(8,128)} copy(f32[512,128]{1,0:T(8,128)} %eigenvalues.1) | data formatting | bytes 524288

commit v3 on v2

--- a/solution.py
+++ b/solution.py
@@ -9,29 +9,30 @@
 MESH = pl.DeviceIdType.MESH
 F32, BF16 = jnp.float32, jnp.bfloat16
 ORDER = (4, 3, -3, 2, -2, 1, -1, 0)
-GROUPS = ((0, 1), (1, 3), (3, 5), (5, 7), (7, 8))
+GROUPS = ((0, 1), (1, 3), (3, 5), (5, 8))
 QS = 4
 WORK = (
-    ("bhop", 1), ("py", 0), ("ahop", 1), ("py", 1), ("bw", 1), ("py", 2), ("bhop", 2), ("aw", 1), ("g",),
-    ("px", 0), ("bw", 2), ("bhop", 3), ("ahop", 2), ("py", 4), ("px", 1), ("px", 2), ("bw", 3), ("pr", 0),
-    ("bhop", 4), ("aw", 2), ("px", 4), ("pr", 1), ("pc", 0), ("bw", 4), ("ahop", 3), ("bs", 0, 0), ("pc", 1),
-    ("bs", 0, 1), ("by", 0), ("aw", 3), ("pw", 0), ("gw",), ("pr", 2), ("py", 3), ("st", 0, 0), ("ahop", 4),
-    ("pc", 2), ("st", 0, 1), ("by", 1), ("pw", 1), ("aw", 4), ("px", 3), ("st", 1, 0), ("ay", 1), ("byw", 0),
-    ("rotA", 0), ("bs", 1, 0), ("pr", 4), ("br", 0, 0), ("st", 1, 1), ("br", 0, 1), ("pr", 3), ("pw", 2),
-    ("st", 2, 0), ("byw", 1), ("ay", 0), ("rotA", 1), ("pc", 4), ("bs", 1, 1), ("pc", 3), ("st", 2, 1),
-    ("pw", 3), ("ayw", 1), ("pw", 4), ("br", 1, 0), ("bl", 0, 1), ("st", 3, 0), ("bl", 0, 0), ("rotA", 2),
-    ("br", 1, 1), ("rotA", 3), ("own",), ("bl", 1, 0), ("st", 3, 1), ("ayw", 0), ("rotB", 2), ("bl", 1, 1),
-    ("rotB", 0), ("rotB", 3), ("rotB", 1), ("sq", 1), ("sq", 0), ("spr", 1), ("spr", 0), ("sq", 3),
-    ("spr", 3), ("sq", 2), ("fin", 1), ("spr", 2), ("fin", 3), ("fin", 0), ("fin", 2),
+    ("py", 1), ("ay",), ("bhop", 1), ("py", 2), ("ahop", 0, 1), ("bw", 1), ("py", 0), ("bhop", 2),
+    ("aw", 0, 1), ("bw", 2), ("bhop", 3), ("g",), ("py", 3), ("px", 0), ("ahop", 0, 2), ("px", 1), ("bw", 3),
+    ("px", 2), ("ayw",), ("ahop", 1, 1), ("aw", 0, 2), ("bhop", 4), ("px", 3), ("ahop", 0, 3), ("pr", 0),
+    ("aw", 1, 1), ("ahop", 1, 2), ("aw", 0, 3), ("bw", 4), ("pr", 1), ("ahop", 0, 4), ("pr", 3), ("bs", 0),
+    ("pr", 2), ("by",), ("aw", 1, 2), ("ahop", 1, 3), ("gw",), ("pc", 0), ("pw", 0), ("st", 0, 0),
+    ("aw", 1, 3), ("pc", 1), ("st", 0, 1), ("pc", 3), ("pw", 1), ("ahop", 1, 4), ("st", 1, 0), ("byw",),
+    ("bs", 1), ("aw", 0, 4), ("pc", 2), ("pw", 3), ("st", 1, 1), ("pw", 2), ("st", 2, 0), ("br", 0),
+    ("rot", 0, 0), ("own",), ("st", 2, 1), ("aw", 1, 4), ("br", 1), ("rot", 1, 0), ("rot", 0, 1),
+    ("st", 3, 0), ("bl", 0), ("rot", 2, 0), ("st", 3, 1), ("bl", 1), ("rot", 1, 1), ("rot", 2, 1),
+    ("rot", 3, 0), ("rot", 3, 1), ("sq", 0), ("sq", 1), ("sq", 3), ("spr", 1), ("sq", 2), ("spr", 0),
+    ("spr", 3), ("spr", 2), ("mid", 1), ("mid", 3), ("mid", 0), ("mid", 2), ("fin", 1), ("fin", 0),
+    ("fin", 3), ("fin", 2),
 )
 
 
 def kernel(
     acts, grads, bout, bin_, slot_seq, seq_len, out,
-    g, bo, bp, a, bi, ra, acc, sb, rb, ownp, sq, cr, ts, tr,
+    g, bo, bp, a, bi, ra, acc, sb, rb, ownp, sq, cr, keep, t1s, t1r, t2s, t2r,
     loc, g_s, g_r, py_s, py_r, px_s, px_r, pc_s, pc_r,
     az_s, az_r, ay_s, ay_r, bz_s, bz_r, by_s, by_r,
-    bx_s, bx_r, bc_s, bc_r, rs_s, rs_r, cs_s, cs_r, ts_s, ts_r,
+    bx_s, bx_r, bc_s, bc_r, rs_s, rs_r, cs_s, cs_r, t1_s, t1_r, t2_s, t2_r,
 ):
     d, t = lax.axis_index("dp"), lax.axis_index("tensor")
     yl, x, c = d // 8, (d // 2) % 4, d % 2
@@ -64,8 +65,7 @@
 
     neighbour = dev(flip_yl=True, flip_yh=True)
     partners = [dev(dz=1), dev(dz=-1), dev(flip_yh=True), neighbour, dev(flip_c=True)]
-    others = [(u, j) for u in range(2) for j in range(4) if u or j]
-    partners += [dev(dx=j, flip_yl=u == 1) for u, j in others]
+    partners += [dev(dx=j) for j in range(1, 4)] + [dev(flip_yl=True)]
     barrier = pltpu.get_barrier_semaphore()
     for to in partners:
         pl.semaphore_signal(barrier, inc=1, device_id=to, device_id_type=MESH)
@@ -81,7 +81,7 @@
         pltpu.make_async_copy(grads, g.at[0], loc.at[10]),
     ]
     local += [pltpu.make_async_copy(bout.at[:, pl.ds(column(k, yh), 512)], bo.at[k], loc.at[k]) for k in range(8)]
-    for copy in local:
+    for copy in local[:2]:
         copy.start()
     pl.semaphore_wait(barrier, len(partners))
 
@@ -98,35 +98,40 @@
         for i in range(2):
             ref = half(bi.at[me, yh, (z - way(i) * h + 8) % 8], i, 64, h)
             arrived(ref, bz_s.at[i, h - 1], bz_r.at[i, h - 1])
+        if h == 1:
+            for copy in local[2:]:
+                copy.start()
         if h == 4:
             local[1].wait()
 
-    def ahop(h):
+    def ahop(u, h):
+        side = 1 - yh if u else yh
         for i in range(2):
             origin = (z - way(i) * (h - 1) + 8) % 8
-            src = a.at[yh, origin] if h > 1 else acts
-            send(half(src, i, 256, h), half(a.at[yh, origin], i, 256, h), az_s.at[i, h - 1], az_r.at[i, h - 1], dev(dz=way(i)))
-
-    def aw(h):
-        for i in range(2):
-            ref = half(a.at[yh, (z - way(i) * h + 8) % 8], i, 256, h)
-            arrived(ref, az_s.at[i, h - 1], az_r.at[i, h - 1])
-        if h == 4:
+            dst = half(a.at[side, origin], i, 256, h)
+            src = acts if h == 1 and u == 0 else dst
+            send(src, dst, az_s.at[u, i, h - 1], az_r.at[u, i, h - 1], dev(dz=way(i)))
+
+    def aw(u, h):
+        side = 1 - yh if u else yh
+        for i in range(2):
+            ref = half(a.at[side, (z - way(i) * h + 8) % 8], i, 256, h)
+            arrived(ref, az_s.at[u, i, h - 1], az_r.at[u, i, h - 1])
+        if u == 0 and h == 4:
             local[0].wait()
 
-    def by(v):
-        ref = bi.at[me, yh, pl.ds(4 * v, 4)]
-        send(ref, ref, by_s.at[v], by_r.at[v], neighbour)
-
-    def byw(v):
-        arrived(bi.at[me, 1 - yh, pl.ds(4 * v, 4)], by_s.at[v], by_r.at[v])
-
-    def ay(v):
-        ref = a.at[yh, pl.ds(4 * v, 4)]
-        send(ref, ref, ay_s.at[v], ay_r.at[v], dev(flip_yh=True))
-
-    def ayw(v):
-        arrived(a.at[1 - yh, pl.ds(4 * v, 4)], ay_s.at[v], ay_r.at[v])
+    def by():
+        ref = bi.at[me, yh]
+        send(ref, ref, by_s, by_r, neighbour)
+
+    def byw():
+        arrived(bi.at[me, 1 - yh], by_s, by_r)
+
+    def ay():
+        send(acts, a.at[yh, z], ay_s, ay_r, dev(flip_yh=True))
+
+    def ayw():
+        arrived(a.at[1 - yh, z], ay_s, ay_r)
 
     def gsend():
         send(grads, g.at[1], g_s, g_r, dev(flip_yh=True))
@@ -173,31 +178,31 @@
     def block(dx, e):
         return (x + dx + 4) % 4 * 2 + e
 
-    def b_part(dx, e, u, v):
-        return bi.at[block(dx, e), 1 - yh if u else yh, pl.ds(4 * v, 4)]
-
-    def to_core(dx, u, v, n):
-        ref = b_part(dx, c, u, v)
-        send(ref, ref, bc_s.at[u, v, n], bc_r.at[u, v, n], dev(flip_c=True))
-
-    def bs(u, v):
-        ref = b_part(0, c, u, v)
-        for i in range(2):
-            send(ref, ref, bx_s.at[u, v, i], bx_r.at[u, v, i], dev(dx=way(i)))
-        to_core(0, u, v, 0)
-
-    def br(u, v):
-        for i in range(2):
-            ref = b_part(-way(i), c, u, v)
-            arrived(ref, bx_s.at[u, v, i], bx_r.at[u, v, i])
-            part = ref.at[pl.ds(2 * i, 2)]
-            send(part, part, bx_s.at[u, v, 2 + i], bx_r.at[u, v, 2 + i], dev(dx=way(i)))
-            to_core(-way(i), u, v, 1 + i)
-
-    def bl(u, v):
-        for i in range(2):
-            arrived(b_part(2, c, u, v).at[pl.ds(2 * i, 2)], bx_s.at[u, v, 2 + i], bx_r.at[u, v, 2 + i])
-        to_core(2, u, v, 3)
+    def b_part(dx, e, u):
+        return bi.at[block(dx, e), 1 - yh if u else yh]
+
+    def to_core(dx, u, n):
+        ref = b_part(dx, c, u)
+        send(ref, ref, bc_s.at[u, n], bc_r.at[u, n], dev(flip_c=True))
+
+    def bs(u):
+        ref = b_part(0, c, u)
+        for i in range(2):
+            send(ref, ref, bx_s.at[u, i], bx_r.at[u, i], dev(dx=way(i)))
+        to_core(0, u, 0)
+
+    def br(u):
+        for i in range(2):
+            ref = b_part(-way(i), c, u)
+            arrived(ref, bx_s.at[u, i], bx_r.at[u, i])
+            part = ref.at[pl.ds(4 * i, 4)]
+            send(part, part, bx_s.at[u, 2 + i], bx_r.at[u, 2 + i], dev(dx=way(i)))
+            to_core(-way(i), u, 1 + i)
+
+    def bl(u):
+        for i in range(2):
+            arrived(b_part(2, c, u).at[pl.ds(4 * i, 4)], bx_s.at[u, 2 + i], bx_r.at[u, 2 + i])
+        to_core(2, u, 3)
 
     def rot_half(b, h):
         left = jnp.concatenate([a[h, k] for k in range(8)], axis=1)
@@ -208,8 +213,7 @@
         for e in (c, 1 - c):
             b = block(dx, e)
             if e is not c:
-                for v in range(2):
-                    arrived(b_part(dx, e, u, v), bc_s.at[u, v, n], bc_r.at[u, v, n])
+                arrived(b_part(dx, e, u), bc_s.at[u, n], bc_r.at[u, n])
             if u == 0:
                 acc[b] = rot_half(b, yh)
             else:
@@ -261,8 +265,6 @@
         for pair in range(2):
             ownp[:, pl.ds(pair * 256, 256)] = product(7, pair)
 
-    blk = yl * 4 + x
-
     def squares(q):
         for i in range(2):
             rs_arrived(i, 3, q)
@@ -278,29 +280,60 @@
             sq[q, 1, b] = total[:, 128:]
         send(sq.at[q, 1 - c], cr.at[q], cs_s.at[q], cs_r.at[q], dev(flip_c=True))
 
-    def chip(u, j):
-        return (1 - yl if u else yl) * 4 + (x + j + 4) % 4
+    def mine(q, y, x_to):
+        b = y * 4 + (x_to + 4) % 4
+        return sq[q, c, b] + cr[q, b]
+
+    def at_x(j):
+        return (x + j + 4) % 4
 
     def spread(q):
         arrived(cr.at[q], cs_s.at[q], cs_r.at[q])
-        for u, j in others:
-            b = chip(u, j)
-            ts[q, b] = (sq[q, c, b] + cr[q, b]).astype(BF16)
-            send(ts.at[q, b], tr.at[q, blk], ts_s.at[q, u, j], ts_r.at[q, u, j], dev(dx=j, flip_yl=u == 1))
+        if q % 2 == 0:
+            for j in range(1, 4):
+                for y in range(2):
+                    t1s[q, at_x(j) * 2 + y] = mine(q, y, at_x(j)).astype(BF16)
+                send(t1s.at[q, pl.ds(at_x(j) * 2, 2)], t1r.at[q, pl.ds(x * 2, 2)], t1_s.at[q, j], t1_r.at[q, j], dev(dx=j))
+        else:
+            for k in range(4):
+                t1s[q, k] = mine(q, 1 - yl, k).astype(BF16)
+            send(t1s.at[q, pl.ds(0, 4)], t1r.at[q, pl.ds(0, 4)], t1_s.at[q, 0], t1_r.at[q, 0], dev(flip_yl=True))
+
+    def middle(q):
+        if q % 2 == 0:
+            for j in range(1, 4):
+                arrived(t1r.at[q, pl.ds(at_x(-j) * 2, 2)], t1_s.at[q, j], t1_r.at[q, j])
+            for y in (1 - yl, yl):
+                total = mine(q, y, x)
+                for j in range(1, 4):
+                    total = total + t1r[q, at_x(-j) * 2 + y].astype(F32)
+                if y is yl:
+                    keep[q] = total
+                else:
+                    t2s[q, 0] = total.astype(BF16)
+                    send(t2s.at[q, 0], t2r.at[q, 0], t2_s.at[q, 0], t2_r.at[q, 0], dev(flip_yl=True))
+        else:
+            arrived(t1r.at[q, pl.ds(0, 4)], t1_s.at[q, 0], t1_r.at[q, 0])
+            for j in range(1, 4):
+                t2s[q, at_x(j)] = (mine(q, yl, at_x(j)) + t1r[q, at_x(j)].astype(F32)).astype(BF16)
+                send(t2s.at[q, at_x(j)], t2r.at[q, x], t2_s.at[q, j], t2_r.at[q, j], dev(dx=j))
+            keep[q] = mine(q, yl, x) + t1r[q, x].astype(F32)
 
     def finish(q):
-        total = sq[q, c, blk] + cr[q, blk]
-        for u, j in others:
-            b = chip(u, -j)
-            arrived(tr.at[q, b], ts_s.at[q, u, j], ts_r.at[q, u, j])
-            total = total + tr[q, b].astype(F32)
+        total = keep[q]
+        if q % 2 == 0:
+            arrived(t2r.at[q, 0], t2_s.at[q, 0], t2_r.at[q, 0])
+            total = total + t2r[q, 0].astype(F32)
+        else:
+            for j in range(1, 4):
+                arrived(t2r.at[q, at_x(-j)], t2_s.at[q, j], t2_r.at[q, j])
+                total = total + t2r[q, at_x(-j)].astype(F32)
         out[pl.ds(q * 128, 128), :] = total * (1.0 / (32 * LEN))
 
     steps = dict(
         bhop=bhop, bw=bw, ahop=ahop, aw=aw, by=by, byw=byw, ay=ay, ayw=ayw, g=gsend, gw=gw,
         py=py, px=px, pr=pr, pc=pc, pw=pw, bs=bs, br=br, bl=bl,
-        rotA=lambda n: rot(n, 0), rotB=lambda n: rot(n, 1), st=st, own=own,
-        sq=squares, spr=spread, fin=finish,
+        rot=rot, st=st, own=own, sq=squares, spr=spread, mid=middle, fin=finish,
     )
     for name, *what in WORK:
         steps[name](*what)
@@ -331,13 +364,16 @@
             pltpu.VMEM((512, 512), F32),
             pltpu.VMEM((QS, 2, 8, 128, 128), F32),
             pltpu.VMEM((QS, 8, 128, 128), F32),
+            pltpu.VMEM((QS, 128, 128), F32),
             pltpu.VMEM((QS, 8, 128, 128), BF16),
             pltpu.VMEM((QS, 8, 128, 128), BF16),
+            pltpu.VMEM((QS, 4, 128, 128), BF16),
+            pltpu.VMEM((QS, 4, 128, 128), BF16),
             sem((11,)),
             *[sem, sem],
-            *pair(8), *pair(5, 4), *pair(5),
-            *pair(2, 4), *pair(2), *pair(2, 4), *pair(2),
-            *pair(2, 2, 4), *pair(2, 2, 4), *pair(2, 4, QS), *pair(QS), *pair(QS, 2, 4),
+            *pair(8), *pair(4, 4), *pair(4),
+            *pair(2, 2, 4), *[sem, sem], *pair(2, 4), *[sem, sem],
+            *pair(2, 4), *pair(2, 4), *pair(2, 4, QS), *pair(QS), *pair(QS, 4), *pair(QS, 4),
         ],
         compiler_params=pltpu.CompilerParams(
             collective_id=0, has_side_effects=True, vmem_limit_bytes=56 << 20

time: 120 us -> 112 us (0.933)
  the two profiles are of different devices: /device:TPU:16 before, /device:TPU:1 now
where the time goes in v3:
time: 112 us
  Pallas kernels  110 us (98%)
  local copies, waits for them, and re-layouts  1.67 us (1%)
    pallas_call x1, Pallas kernels, shards(): pl.pallas_call(kernel, name='eigenvalues', out_shape=jax.ShapeDtypeStruct...  110 us

profile of v3, /device:TPU:1, one launch (start us, length us, event | category | flops | bytes accessed | tf_op | source)
XLA Modules:
  0.0 111.8 jit_solution(625482189620030569)
XLA Ops:
  0.0 110.2 %eigenvalues.1 = f32[512,128]{1,0:T(8,128)} custom-call(bf16[512,128]{1,0:T(8,128)(2,1)} %acts.1, bf16[512,512]{1,0:T(8,128)(2,1)} %grads.1, bf16[512,8192]{1,0:T(8,128)(2,1)} %bout.1, bf16[128,2048]{1,0:T(8,128)(2,1)} %bin_.1, s32[32]{0:T(128)} %slot_seq.1, s32[32]{0:T(128)} %seq_len.1), custom_call_target="tpu_custom_call" | custom-call | flops 10737418240 | bytes 12582912 | tf_op jit(solution)/shard_map/eigenvalues/pallas_call | solution.py:348
  110.2 1.7 %copy.8 = f32[512,128]{1,0:T(8,128)} copy(f32[512,128]{1,0:T(8,128)} %eigenvalues.1) | data formatting | bytes 524288

commit v4 on v3

--- a/solution.py
+++ b/solution.py
@@ -12,24 +12,23 @@
 GROUPS = ((0, 1), (1, 3), (3, 5), (5, 8))
 QS = 4
 WORK = (
-    ("py", 1), ("ay",), ("bhop", 1), ("py", 2), ("ahop", 0, 1), ("bw", 1), ("py", 0), ("bhop", 2),
-    ("aw", 0, 1), ("bw", 2), ("bhop", 3), ("g",), ("py", 3), ("px", 0), ("ahop", 0, 2), ("px", 1), ("bw", 3),
-    ("px", 2), ("ayw",), ("ahop", 1, 1), ("aw", 0, 2), ("bhop", 4), ("px", 3), ("ahop", 0, 3), ("pr", 0),
-    ("aw", 1, 1), ("ahop", 1, 2), ("aw", 0, 3), ("bw", 4), ("pr", 1), ("ahop", 0, 4), ("pr", 3), ("bs", 0),
-    ("pr", 2), ("by",), ("aw", 1, 2), ("ahop", 1, 3), ("gw",), ("pc", 0), ("pw", 0), ("st", 0, 0),
-    ("aw", 1, 3), ("pc", 1), ("st", 0, 1), ("pc", 3), ("pw", 1), ("ahop", 1, 4), ("st", 1, 0), ("byw",),
-    ("bs", 1), ("aw", 0, 4), ("pc", 2), ("pw", 3), ("st", 1, 1), ("pw", 2), ("st", 2, 0), ("br", 0),
-    ("rot", 0, 0), ("own",), ("st", 2, 1), ("aw", 1, 4), ("br", 1), ("rot", 1, 0), ("rot", 0, 1),
-    ("st", 3, 0), ("bl", 0), ("rot", 2, 0), ("st", 3, 1), ("bl", 1), ("rot", 1, 1), ("rot", 2, 1),
-    ("rot", 3, 0), ("rot", 3, 1), ("sq", 0), ("sq", 1), ("sq", 3), ("spr", 1), ("sq", 2), ("spr", 0),
-    ("spr", 3), ("spr", 2), ("mid", 1), ("mid", 3), ("mid", 0), ("mid", 2), ("fin", 1), ("fin", 0),
-    ("fin", 3), ("fin", 2),
+    ("ay",), ("py", 0), ("bhop", 1), ("ahop", 0, 1), ("py", 2), ("py", 1), ("bw", 1), ("bhop", 2), ("py", 3),
+    ("ayw",), ("ahop", 1, 1), ("px", 0), ("aw", 0, 1), ("bw", 2), ("bhop", 3), ("g",), ("ahop", 0, 2),
+    ("px", 2), ("px", 1), ("bw", 3), ("aw", 1, 1), ("pr", 0), ("bhop", 4), ("ahop", 1, 2), ("aw", 0, 2),
+    ("px", 3), ("pr", 2), ("bw", 4), ("pc", 0), ("ahop", 0, 3), ("pr", 1), ("by",), ("aw", 1, 2), ("bs", 0),
+    ("ahop", 1, 3), ("pw", 0), ("aw", 0, 3), ("gw",), ("st", 0, 0), ("pc", 1), ("st", 0, 1), ("pr", 3),
+    ("pc", 2), ("aw", 1, 3), ("ahop", 0, 4), ("ahop", 1, 4), ("pw", 2), ("pw", 1), ("st", 1, 0), ("byw",),
+    ("bs", 1), ("br", 0), ("aw", 0, 4), ("st", 1, 1), ("aw", 1, 4), ("st", 2, 0), ("rot", 2, 0), ("pc", 3),
+    ("st", 2, 1), ("pw", 3), ("br", 1), ("rot", 0, 0), ("rot", 1, 0), ("st", 3, 0), ("own",), ("rot", 2, 1),
+    ("bl", 0), ("rot", 0, 1), ("st", 3, 1), ("bl", 1), ("rot", 1, 1), ("rot", 3, 0), ("rot", 3, 1), ("sq", 0),
+    ("sq", 1), ("sq", 2), ("spr", 0), ("sq", 3), ("spr", 1), ("spr", 2), ("spr", 3), ("mid", 1), ("mid", 0),
+    ("mid", 3), ("mid", 2), ("fin", 1), ("fin", 0), ("fin", 2), ("fin", 3),
 )
 
 
 def kernel(
     acts, grads, bout, bin_, slot_seq, seq_len, out,
-    g, bo, bp, a, bi, ra, acc, sb, rb, ownp, sq, cr, keep, t1s, t1r, t2s, t2r,
+    g, bo, bp, a, bi, ra, acc, sb, rb, ownp, sq, cr, keep, t1s, t1r, t2s, t2r, t3s, t3r,
     loc, g_s, g_r, py_s, py_r, px_s, px_r, pc_s, pc_r,
     az_s, az_r, ay_s, ay_r, bz_s, bz_r, by_s, by_r,
     bx_s, bx_r, bc_s, bc_r, rs_s, rs_r, cs_s, cs_r, t1_s, t1_r, t2_s, t2_r,
@@ -310,8 +309,8 @@
                 if y is yl:
                     keep[q] = total
                 else:
-                    t2s[q, 0] = total.astype(BF16)
-                    send(t2s.at[q, 0], t2r.at[q, 0], t2_s.at[q, 0], t2_r.at[q, 0], dev(flip_yl=True))
+                    t3s[q] = total
+                    send(t3s.at[q], t3r.at[q], t2_s.at[q, 0], t2_r.at[q, 0], dev(flip_yl=True))
         else:
             arrived(t1r.at[q, pl.ds(0, 4)], t1_s.at[q, 0], t1_r.at[q, 0])
             for j in range(1, 4):
@@ -322,8 +321,8 @@
     def finish(q):
         total = keep[q]
         if q % 2 == 0:
-            arrived(t2r.at[q, 0], t2_s.at[q, 0], t2_r.at[q, 0])
-            total = total + t2r[q, 0].astype(F32)
+            arrived(t3r.at[q], t2_s.at[q, 0], t2_r.at[q, 0])
+            total = total + t3r[q]
         else:
             for j in range(1, 4):
                 arrived(t2r.at[q, at_x(-j)], t2_s.at[q, j], t2_r.at[q, j])
@@ -369,6 +368,8 @@
             pltpu.VMEM((QS, 8, 128, 128), BF16),
             pltpu.VMEM((QS, 4, 128, 128), BF16),
             pltpu.VMEM((QS, 4, 128, 128), BF16),
+            pltpu.VMEM((QS, 128, 128), F32),
+            pltpu.VMEM((QS, 128, 128), F32),
             sem((11,)),
             *[sem, sem],
             *pair(8), *pair(4, 4), *pair(4),

time: 112 us -> 105 us (0.938)
  Pallas kernels: 110 us -> 103 us
    pallas_call x1, Pallas kernels: 110 us -> 103 us  [shards(): pl.pallas_call(kernel, name='eigenvalues', out_shape=jax.ShapeDtypeStruct...]
where the time goes in v4:
time: 105 us
  Pallas kernels  103 us (98%)
  local copies, waits for them, and re-layouts  1.67 us (2%)
    pallas_call x1, Pallas kernels, shards(): pl.pallas_call(kernel, name='eigenvalues', out_shape=jax.ShapeDtypeStruct...  103 us

profile of v4, /device:TPU:1, one launch (start us, length us, event | category | flops | bytes accessed | tf_op | source)
XLA Modules:
  0.0 104.6 jit_solution(7767444066278106160)
XLA Ops:
  0.0 103.0 %eigenvalues.1 = f32[512,128]{1,0:T(8,128)} custom-call(bf16[512,128]{1,0:T(8,128)(2,1)} %acts.1, bf16[512,512]{1,0:T(8,128)(2,1)} %grads.1, bf16[512,8192]{1,0:T(8,128)(2,1)} %bout.1, bf16[128,2048]{1,0:T(8,128)(2,1)} %bin_.1, s32[32]{0:T(128)} %slot_seq.1, s32[32]{0:T(128)} %seq_len.1), custom_call_target="tpu_custom_call" | custom-call | flops 10737418240 | bytes 12582912 | tf_op jit(solution)/shard_map/eigenvalues/pallas_call | solution.py:347
  103.0 1.7 %copy.8 = f32[512,128]{1,0:T(8,128)} copy(f32[512,128]{1,0:T(8,128)} %eigenvalues.1) | data formatting | bytes 524288

commit v5 on v4

--- a/solution.py
+++ b/solution.py
@@ -12,17 +12,17 @@
 GROUPS = ((0, 1), (1, 3), (3, 5), (5, 8))
 QS = 4
 WORK = (
-    ("ay",), ("py", 0), ("bhop", 1), ("ahop", 0, 1), ("py", 2), ("py", 1), ("bw", 1), ("bhop", 2), ("py", 3),
-    ("ayw",), ("ahop", 1, 1), ("px", 0), ("aw", 0, 1), ("bw", 2), ("bhop", 3), ("g",), ("ahop", 0, 2),
-    ("px", 2), ("px", 1), ("bw", 3), ("aw", 1, 1), ("pr", 0), ("bhop", 4), ("ahop", 1, 2), ("aw", 0, 2),
-    ("px", 3), ("pr", 2), ("bw", 4), ("pc", 0), ("ahop", 0, 3), ("pr", 1), ("by",), ("aw", 1, 2), ("bs", 0),
-    ("ahop", 1, 3), ("pw", 0), ("aw", 0, 3), ("gw",), ("st", 0, 0), ("pc", 1), ("st", 0, 1), ("pr", 3),
-    ("pc", 2), ("aw", 1, 3), ("ahop", 0, 4), ("ahop", 1, 4), ("pw", 2), ("pw", 1), ("st", 1, 0), ("byw",),
-    ("bs", 1), ("br", 0), ("aw", 0, 4), ("st", 1, 1), ("aw", 1, 4), ("st", 2, 0), ("rot", 2, 0), ("pc", 3),
-    ("st", 2, 1), ("pw", 3), ("br", 1), ("rot", 0, 0), ("rot", 1, 0), ("st", 3, 0), ("own",), ("rot", 2, 1),
-    ("bl", 0), ("rot", 0, 1), ("st", 3, 1), ("bl", 1), ("rot", 1, 1), ("rot", 3, 0), ("rot", 3, 1), ("sq", 0),
-    ("sq", 1), ("sq", 2), ("spr", 0), ("sq", 3), ("spr", 1), ("spr", 2), ("spr", 3), ("mid", 1), ("mid", 0),
-    ("mid", 3), ("mid", 2), ("fin", 1), ("fin", 0), ("fin", 2), ("fin", 3),
+    ("py", 0), ("bhop", 1), ("py", 1), ("py", 2), ("ahop", 1), ("g",), ("px", 0), ("bw", 1), ("bhop", 2),
+    ("px", 1), ("bw", 2), ("bhop", 3), ("px", 2), ("aw", 1), ("pr", 0), ("py", 3), ("ahop", 2), ("bw", 3),
+    ("bhop", 4), ("pr", 1), ("aw", 2), ("pr", 2), ("bw", 4), ("bs", 0, 0), ("ahop", 3), ("by", 0), ("pc", 0),
+    ("pw", 0), ("gw",), ("st", 0, 0), ("pc", 1), ("pc", 2), ("by", 1), ("px", 3), ("aw", 3), ("ahop", 4),
+    ("pw", 1), ("st", 0, 1), ("bs", 0, 1), ("st", 1, 0), ("pr", 3), ("pw", 2), ("byw", 0), ("aw", 4),
+    ("ay", 1), ("bs", 1, 0), ("ay", 0), ("st", 1, 1), ("byw", 1), ("br", 0, 0), ("st", 2, 0), ("pc", 3),
+    ("bs", 1, 1), ("rot", 0, 0), ("br", 0, 1), ("st", 2, 1), ("rot", 2, 0), ("rot", 1, 0), ("br", 1, 0),
+    ("pw", 3), ("st", 3, 0), ("br", 1, 1), ("bl", 0, 0), ("ayw", 1), ("own",), ("st", 3, 1), ("bl", 0, 1),
+    ("ayw", 0), ("rot", 1, 1), ("rot", 2, 1), ("bl", 1, 1), ("bl", 1, 0), ("rot", 0, 1), ("rot", 3, 0),
+    ("rot", 3, 1), ("sq", 0), ("sq", 3), ("sq", 1), ("sq", 2), ("spr", 3), ("spr", 0), ("spr", 2), ("spr", 1),
+    ("mid", 3), ("mid", 1), ("mid", 0), ("mid", 2), ("fin", 3), ("fin", 0), ("fin", 1), ("fin", 2),
 )
 
 
@@ -103,34 +103,32 @@
         if h == 4:
             local[1].wait()
 
-    def ahop(u, h):
-        side = 1 - yh if u else yh
+    def ahop(h):
         for i in range(2):
             origin = (z - way(i) * (h - 1) + 8) % 8
-            dst = half(a.at[side, origin], i, 256, h)
-            src = acts if h == 1 and u == 0 else dst
-            send(src, dst, az_s.at[u, i, h - 1], az_r.at[u, i, h - 1], dev(dz=way(i)))
-
-    def aw(u, h):
-        side = 1 - yh if u else yh
-        for i in range(2):
-            ref = half(a.at[side, (z - way(i) * h + 8) % 8], i, 256, h)
-            arrived(ref, az_s.at[u, i, h - 1], az_r.at[u, i, h - 1])
-        if u == 0 and h == 4:
+            src = a.at[yh, origin] if h > 1 else acts
+            send(half(src, i, 256, h), half(a.at[yh, origin], i, 256, h), az_s.at[i, h - 1], az_r.at[i, h - 1], dev(dz=way(i)))
+
+    def aw(h):
+        for i in range(2):
+            ref = half(a.at[yh, (z - way(i) * h + 8) % 8], i, 256, h)
+            arrived(ref, az_s.at[i, h - 1], az_r.at[i, h - 1])
+        if h == 4:
             local[0].wait()
 
-    def by():
-        ref = bi.at[me, yh]
-        send(ref, ref, by_s, by_r, neighbour)
-
-    def byw():
-        arrived(bi.at[me, 1 - yh], by_s, by_r)
-
-    def ay():
-        send(acts, a.at[yh, z], ay_s, ay_r, dev(flip_yh=True))
-
-    def ayw():
-        arrived(a.at[1 - yh, z], ay_s, ay_r)
+    def by(v):
+        ref = bi.at[me, yh, pl.ds(4 * v, 4)]
+        send(ref, ref, by_s.at[v], by_r.at[v], neighbour)
+
+    def byw(v):
+        arrived(bi.at[me, 1 - yh, pl.ds(4 * v, 4)], by_s.at[v], by_r.at[v])
+
+    def ay(v):
+        ref = a.at[yh, pl.ds(4 * v, 4)]
+        send(ref, ref, ay_s.at[v], ay_r.at[v], dev(flip_yh=True))
+
+    def ayw(v):
+        arrived(a.at[1 - yh, pl.ds(4 * v, 4)], ay_s.at[v], ay_r.at[v])
 
     def gsend():
         send(grads, g.at[1], g_s, g_r, dev(flip_yh=True))
@@ -177,31 +175,31 @@
     def block(dx, e):
         return (x + dx + 4) % 4 * 2 + e
 
-    def b_part(dx, e, u):
-        return bi.at[block(dx, e), 1 - yh if u else yh]
-
-    def to_core(dx, u, n):
-        ref = b_part(dx, c, u)
-        send(ref, ref, bc_s.at[u, n], bc_r.at[u, n], dev(flip_c=True))
-
-    def bs(u):
-        ref = b_part(0, c, u)
-        for i in range(2):
-            send(ref, ref, bx_s.at[u, i], bx_r.at[u, i], dev(dx=way(i)))
-        to_core(0, u, 0)
-
-    def br(u):
-        for i in range(2):
-            ref = b_part(-way(i), c, u)
-            arrived(ref, bx_s.at[u, i], bx_r.at[u, i])
-            part = ref.at[pl.ds(4 * i, 4)]
-            send(part, part, bx_s.at[u, 2 + i], bx_r.at[u, 2 + i], dev(dx=way(i)))
-            to_core(-way(i), u, 1 + i)
-
-    def bl(u):
-        for i in range(2):
-            arrived(b_part(2, c, u).at[pl.ds(4 * i, 4)], bx_s.at[u, 2 + i], bx_r.at[u, 2 + i])
-        to_core(2, u, 3)
+    def b_part(dx, e, u, v):
+        return bi.at[block(dx, e), 1 - yh if u else yh, pl.ds(4 * v, 4)]
+
+    def to_core(dx, u, v, n):
+        ref = b_part(dx, c, u, v)
+        send(ref, ref, bc_s.at[u, v, n], bc_r.at[u, v, n], dev(flip_c=True))
+
+    def bs(u, v):
+        ref = b_part(0, c, u, v)
+        for i in range(2):
+            send(ref, ref, bx_s.at[u, v, i], bx_r.at[u, v, i], dev(dx=way(i)))
+        to_core(0, u, v, 0)
+
+    def br(u, v):
+        for i in range(2):
+            ref = b_part(-way(i), c, u, v)
+            arrived(ref, bx_s.at[u, v, i], bx_r.at[u, v, i])
+            part = ref.at[pl.ds(2 * i, 2)]
+            send(part, part, bx_s.at[u, v, 2 + i], bx_r.at[u, v, 2 + i], dev(dx=way(i)))
+            to_core(-way(i), u, v, 1 + i)
+
+    def bl(u, v):
+        for i in range(2):
+            arrived(b_part(2, c, u, v).at[pl.ds(2 * i, 2)], bx_s.at[u, v, 2 + i], bx_r.at[u, v, 2 + i])
+        to_core(2, u, v, 3)
 
     def rot_half(b, h):
         left = jnp.concatenate([a[h, k] for k in range(8)], axis=1)
@@ -212,7 +210,8 @@
         for e in (c, 1 - c):
             b = block(dx, e)
             if e is not c:
-                arrived(b_part(dx, e, u), bc_s.at[u, n], bc_r.at[u, n])
+                for v in range(2):
+                    arrived(b_part(dx, e, u, v), bc_s.at[u, v, n], bc_r.at[u, v, n])
             if u == 0:
                 acc[b] = rot_half(b, yh)
             else:
@@ -373,8 +372,8 @@
             sem((11,)),
             *[sem, sem],
             *pair(8), *pair(4, 4), *pair(4),
-            *pair(2, 2, 4), *[sem, sem], *pair(2, 4), *[sem, sem],
-            *pair(2, 4), *pair(2, 4), *pair(2, 4, QS), *pair(QS), *pair(QS, 4), *pair(QS, 4),
+            *pair(2, 4), *pair(2), *pair(2, 4), *pair(2),
+            *pair(2, 2, 4), *pair(2, 2, 4), *pair(2, 4, QS), *pair(QS), *pair(QS, 4), *pair(QS, 4),
         ],
         compiler_params=pltpu.CompilerParams(
             collective_id=0, has_side_effects=True, vmem_limit_bytes=56 << 20

time: 105 us -> 110 us (1.048)
  Pallas kernels: 103 us -> 108 us
    pallas_call x1, Pallas kernels: 103 us -> 108 us  [shards(): pl.pallas_call(kernel, name='eigenvalues', out_shape=jax.ShapeDtypeStruct...]
where the time goes in v5:
time: 110 us
  Pallas kernels  108 us (98%)
  local copies, waits for them, and re-layouts  1.67 us (2%)
    pallas_call x1, Pallas kernels, shards(): pl.pallas_call(kernel, name='eigenvalues', out_shape=jax.ShapeDtypeStruct...  108 us

profile of v5, /device:TPU:1, one launch (start us, length us, event | category | flops | bytes accessed | tf_op | source)
XLA Modules:
  0.0 110.0 jit_solution(4897731754084942677)
XLA Ops:
  0.0 108.3 %eigenvalues.1 = f32[512,128]{1,0:T(8,128)} custom-call(bf16[512,128]{1,0:T(8,128)(2,1)} %acts.1, bf16[512,512]{1,0:T(8,128)(2,1)} %grads.1, bf16[512,8192]{1,0:T(8,128)(2,1)} %bout.1, bf16[128,2048]{1,0:T(8,128)(2,1)} %bin_.1, s32[32]{0:T(128)} %slot_seq.1, s32[32]{0:T(128)} %seq_len.1), custom_call_target="tpu_custom_call" | custom-call | flops 10737418240 | bytes 12582912 | tf_op jit(solution)/shard_map/eigenvalues/pallas_call | solution.py:346
  108.3 1.7 %copy.8 = f32[512,128]{1,0:T(8,128)} copy(f32[512,128]{1,0:T(8,128)} %eigenvalues.1) | data formatting | bytes 524288

commit v6 on v5

--- a/solution.py
+++ b/solution.py
@@ -12,17 +12,19 @@
 GROUPS = ((0, 1), (1, 3), (3, 5), (5, 8))
 QS = 4
 WORK = (
-    ("py", 0), ("bhop", 1), ("py", 1), ("py", 2), ("ahop", 1), ("g",), ("px", 0), ("bw", 1), ("bhop", 2),
-    ("px", 1), ("bw", 2), ("bhop", 3), ("px", 2), ("aw", 1), ("pr", 0), ("py", 3), ("ahop", 2), ("bw", 3),
-    ("bhop", 4), ("pr", 1), ("aw", 2), ("pr", 2), ("bw", 4), ("bs", 0, 0), ("ahop", 3), ("by", 0), ("pc", 0),
-    ("pw", 0), ("gw",), ("st", 0, 0), ("pc", 1), ("pc", 2), ("by", 1), ("px", 3), ("aw", 3), ("ahop", 4),
-    ("pw", 1), ("st", 0, 1), ("bs", 0, 1), ("st", 1, 0), ("pr", 3), ("pw", 2), ("byw", 0), ("aw", 4),
-    ("ay", 1), ("bs", 1, 0), ("ay", 0), ("st", 1, 1), ("byw", 1), ("br", 0, 0), ("st", 2, 0), ("pc", 3),
-    ("bs", 1, 1), ("rot", 0, 0), ("br", 0, 1), ("st", 2, 1), ("rot", 2, 0), ("rot", 1, 0), ("br", 1, 0),
-    ("pw", 3), ("st", 3, 0), ("br", 1, 1), ("bl", 0, 0), ("ayw", 1), ("own",), ("st", 3, 1), ("bl", 0, 1),
-    ("ayw", 0), ("rot", 1, 1), ("rot", 2, 1), ("bl", 1, 1), ("bl", 1, 0), ("rot", 0, 1), ("rot", 3, 0),
-    ("rot", 3, 1), ("sq", 0), ("sq", 3), ("sq", 1), ("sq", 2), ("spr", 3), ("spr", 0), ("spr", 2), ("spr", 1),
-    ("mid", 3), ("mid", 1), ("mid", 0), ("mid", 2), ("fin", 3), ("fin", 0), ("fin", 1), ("fin", 2),
+    ("py", 0), ("bhop", 1), ("py", 1), ("ahop", 0, 1), ("py", 2), ("bw", 1), ("ay",), ("bhop", 2), ("px", 0),
+    ("px", 1), ("g",), ("bw", 2), ("bhop", 3), ("aw", 0, 1), ("ahop", 0, 2), ("px", 2), ("bw", 3),
+    ("bhop", 4), ("pr", 0), ("ayw",), ("ahop", 1, 1), ("pr", 1), ("py", 3), ("pr", 2), ("aw", 0, 2),
+    ("ahop", 0, 3), ("bw", 4), ("bs", 0, 0), ("bs", 0, 1), ("by", 0), ("by", 1), ("aw", 1, 1), ("pc", 0),
+    ("ahop", 1, 2), ("pw", 0), ("aw", 0, 3), ("ahop", 0, 4), ("gw",), ("st", 0, 0), ("pc", 1), ("st", 0, 1),
+    ("px", 3), ("aw", 1, 2), ("ahop", 1, 3), ("pw", 1), ("st", 1, 0), ("pc", 2), ("st", 1, 1), ("byw", 0),
+    ("pr", 3), ("byw", 1), ("bs", 1, 0), ("bs", 1, 1), ("br", 0, 0), ("br", 0, 1), ("aw", 1, 3), ("aw", 0, 4),
+    ("ah",), ("pw", 2), ("st", 2, 0), ("ahop", 1, 4), ("rot", 0, 0), ("pc", 3), ("pw", 3), ("st", 2, 1),
+    ("rot", 2, 0), ("st", 3, 0), ("br", 1, 0), ("br", 1, 1), ("rot", 1, 0), ("own",), ("aw", 1, 4), ("ahw",),
+    ("rot", 1, 1), ("st", 3, 1), ("bl", 0, 0), ("bl", 0, 1), ("rot", 2, 1), ("rot", 0, 1), ("bl", 1, 0),
+    ("bl", 1, 1), ("rot", 3, 0), ("rot", 3, 1), ("sq", 1), ("sq", 2), ("sq", 0), ("sq", 3), ("spr", 1),
+    ("spr", 2), ("spr", 3), ("spr", 0), ("mid", 1), ("mid", 2), ("mid", 3), ("mid", 0), ("fin", 1),
+    ("fin", 2), ("fin", 3), ("fin", 0),
 )
 
 
@@ -30,7 +32,7 @@
     acts, grads, bout, bin_, slot_seq, seq_len, out,
     g, bo, bp, a, bi, ra, acc, sb, rb, ownp, sq, cr, keep, t1s, t1r, t2s, t2r, t3s, t3r,
     loc, g_s, g_r, py_s, py_r, px_s, px_r, pc_s, pc_r,
-    az_s, az_r, ay_s, ay_r, bz_s, bz_r, by_s, by_r,
+    az_s, az_r, ay_s, ay_r, ah_s, ah_r, bz_s, bz_r, by_s, by_r,
     bx_s, bx_r, bc_s, bc_r, rs_s, rs_r, cs_s, cs_r, t1_s, t1_r, t2_s, t2_r,
 ):
     d, t = lax.axis_index("dp"), lax.axis_index("tensor")
@@ -103,17 +105,20 @@
         if h == 4:
             local[1].wait()
 
-    def ahop(h):
+    def ahop(u, h):
+        side, size = (1 - yh, 256) if u else (yh, 512)
         for i in range(2):
             origin = (z - way(i) * (h - 1) + 8) % 8
-            src = a.at[yh, origin] if h > 1 else acts
-            send(half(src, i, 256, h), half(a.at[yh, origin], i, 256, h), az_s.at[i, h - 1], az_r.at[i, h - 1], dev(dz=way(i)))
-
-    def aw(h):
-        for i in range(2):
-            ref = half(a.at[yh, (z - way(i) * h + 8) % 8], i, 256, h)
-            arrived(ref, az_s.at[i, h - 1], az_r.at[i, h - 1])
-        if h == 4:
+            dst = half(a.at[side, origin, pl.ds(0, size)], i, size // 2, h)
+            src = acts if h == 1 and u == 0 else dst
+            send(src, dst, az_s.at[u, i, h - 1], az_r.at[u, i, h - 1], dev(dz=way(i)))
+
+    def aw(u, h):
+        side, size = (1 - yh, 256) if u else (yh, 512)
+        for i in range(2):
+            ref = half(a.at[side, (z - way(i) * h + 8) % 8, pl.ds(0, size)], i, size // 2, h)
+            arrived(ref, az_s.at[u, i, h - 1], az_r.at[u, i, h - 1])
+        if u == 0 and h == 4:
             local[0].wait()
 
     def by(v):
@@ -123,12 +128,18 @@
     def byw(v):
         arrived(bi.at[me, 1 - yh, pl.ds(4 * v, 4)], by_s.at[v], by_r.at[v])
 
-    def ay(v):
-        ref = a.at[yh, pl.ds(4 * v, 4)]
-        send(ref, ref, ay_s.at[v], ay_r.at[v], dev(flip_yh=True))
-
-    def ayw(v):
-        arrived(a.at[1 - yh, pl.ds(4 * v, 4)], ay_s.at[v], ay_r.at[v])
+    def ay():
+        send(acts.at[pl.ds(0, 256)], a.at[yh, z, pl.ds(0, 256)], ay_s, ay_r, dev(flip_yh=True))
+
+    def ayw():
+        arrived(a.at[1 - yh, z, pl.ds(0, 256)], ay_s, ay_r)
+
+    def ah():
+        ref = a.at[yh, pl.ds(0, 8), pl.ds(256, 256)]
+        send(ref, ref, ah_s, ah_r, dev(flip_yh=True))
+
+    def ahw():
+        arrived(a.at[1 - yh, pl.ds(0, 8), pl.ds(256, 256)], ah_s, ah_r)
 
     def gsend():
         send(grads, g.at[1], g_s, g_r, dev(flip_yh=True))
@@ -329,7 +340,7 @@
         out[pl.ds(q * 128, 128), :] = total * (1.0 / (32 * LEN))
 
     steps = dict(
-        bhop=bhop, bw=bw, ahop=ahop, aw=aw, by=by, byw=byw, ay=ay, ayw=ayw, g=gsend, gw=gw,
+        bhop=bhop, bw=bw, ahop=ahop, aw=aw, by=by, byw=byw, ay=ay, ayw=ayw, ah=ah, ahw=ahw, g=gsend, gw=gw,
         py=py, px=px, pr=pr, pc=pc, pw=pw, bs=bs, br=br, bl=bl,
         rot=rot, st=st, own=own, sq=squares, spr=spread, mid=middle, fin=finish,
     )
@@ -372,7 +383,7 @@
             sem((11,)),
             *[sem, sem],
             *pair(8), *pair(4, 4), *pair(4),
-            *pair(2, 4), *pair(2), *pair(2, 4), *pair(2),
+            *pair(2, 2, 4), *[sem] * 4, *pair(2, 4), *pair(2),
             *pair(2, 2, 4), *pair(2, 2, 4), *pair(2, 4, QS), *pair(QS), *pair(QS, 4), *pair(QS, 4),
         ],
         compiler_params=pltpu.CompilerParams(

time: 110 us -> 105 us (0.955)
  Pallas kernels: 108 us -> 103 us
    pallas_call x1, Pallas kernels: 108 us -> 103 us  [shards(): pl.pallas_call(kernel, name='eigenvalues', out_shape=jax.ShapeDtypeStruct...]
where the time goes in v6:
time: 105 us
  Pallas kernels  103 us (98%)
  local copies, waits for them, and re-layouts  1.67 us (2%)
    pallas_call x1, Pallas kernels, shards(): pl.pallas_call(kernel, name='eigenvalues', out_shape=jax.ShapeDtypeStruct...  103 us

profile of v6, /device:TPU:1, one launch (start us, length us, event | category | flops | bytes accessed | tf_op | source)
XLA Modules:
  0.0 104.8 jit_solution(15360085490602967554)
XLA Ops:
  0.0 103.1 %eigenvalues.1 = f32[512,128]{1,0:T(8,128)} custom-call(bf16[512,128]{1,0:T(8,128)(2,1)} %acts.1, bf16[512,512]{1,0:T(8,128)(2,1)} %grads.1, bf16[512,8192]{1,0:T(8,128)(2,1)} %bout.1, bf16[128,2048]{1,0:T(8,128)(2,1)} %bin_.1, s32[32]{0:T(128)} %slot_seq.1, s32[32]{0:T(128)} %seq_len.1), custom_call_target="tpu_custom_call" | custom-call | flops 10737418240 | bytes 12582912 | tf_op jit(solution)/shard_map/eigenvalues/pallas_call | solution.py:357
  103.1 1.7 %copy.8 = f32[512,128]{1,0:T(8,128)} copy(f32[512,128]{1,0:T(8,128)} %eigenvalues.1) | data formatting | bytes 524288

commit v7 on v4

--- a/solution.py
+++ b/solution.py
@@ -12,17 +12,17 @@
 GROUPS = ((0, 1), (1, 3), (3, 5), (5, 8))
 QS = 4
 WORK = (
-    ("ay",), ("py", 0), ("bhop", 1), ("ahop", 0, 1), ("py", 2), ("py", 1), ("bw", 1), ("bhop", 2), ("py", 3),
-    ("ayw",), ("ahop", 1, 1), ("px", 0), ("aw", 0, 1), ("bw", 2), ("bhop", 3), ("g",), ("ahop", 0, 2),
-    ("px", 2), ("px", 1), ("bw", 3), ("aw", 1, 1), ("pr", 0), ("bhop", 4), ("ahop", 1, 2), ("aw", 0, 2),
-    ("px", 3), ("pr", 2), ("bw", 4), ("pc", 0), ("ahop", 0, 3), ("pr", 1), ("by",), ("aw", 1, 2), ("bs", 0),
-    ("ahop", 1, 3), ("pw", 0), ("aw", 0, 3), ("gw",), ("st", 0, 0), ("pc", 1), ("st", 0, 1), ("pr", 3),
-    ("pc", 2), ("aw", 1, 3), ("ahop", 0, 4), ("ahop", 1, 4), ("pw", 2), ("pw", 1), ("st", 1, 0), ("byw",),
-    ("bs", 1), ("br", 0), ("aw", 0, 4), ("st", 1, 1), ("aw", 1, 4), ("st", 2, 0), ("rot", 2, 0), ("pc", 3),
-    ("st", 2, 1), ("pw", 3), ("br", 1), ("rot", 0, 0), ("rot", 1, 0), ("st", 3, 0), ("own",), ("rot", 2, 1),
-    ("bl", 0), ("rot", 0, 1), ("st", 3, 1), ("bl", 1), ("rot", 1, 1), ("rot", 3, 0), ("rot", 3, 1), ("sq", 0),
-    ("sq", 1), ("sq", 2), ("spr", 0), ("sq", 3), ("spr", 1), ("spr", 2), ("spr", 3), ("mid", 1), ("mid", 0),
-    ("mid", 3), ("mid", 2), ("fin", 1), ("fin", 0), ("fin", 2), ("fin", 3),
+    ("py", 0), ("py", 2), ("bhop", 1), ("py", 1), ("ahop", 0, 1), ("bw", 1), ("bhop", 2), ("ay",), ("px", 0),
+    ("g",), ("py", 3), ("px", 2), ("bw", 2), ("bhop", 3), ("aw", 0, 1), ("ahop", 0, 2), ("px", 1), ("pr", 0),
+    ("bw", 3), ("bhop", 4), ("ayw",), ("ahop", 1, 1), ("pr", 2), ("bw", 4), ("aw", 0, 2), ("pr", 1),
+    ("ahop", 0, 3), ("pc", 2), ("aw", 1, 1), ("pc", 0), ("by",), ("ahop", 1, 2), ("bs", 0), ("pc", 1),
+    ("aw", 0, 3), ("ahop", 0, 4), ("pw", 0), ("aw", 1, 2), ("ahop", 1, 3), ("gw",), ("st", 0, 0),
+    ("aw", 0, 4), ("st", 0, 1), ("px", 3), ("pw", 2), ("br", 0), ("pw", 1), ("aw", 1, 3), ("ahop", 1, 4),
+    ("st", 1, 0), ("pr", 3), ("st", 1, 1), ("byw",), ("bs", 1), ("rot", 1, 0), ("st", 2, 0), ("bl", 0),
+    ("aw", 1, 4), ("st", 2, 1), ("pc", 3), ("rot", 0, 0), ("pw", 3), ("br", 1), ("st", 3, 0), ("rot", 1, 1),
+    ("rot", 0, 1), ("st", 3, 1), ("own",), ("rot", 2, 0), ("bl", 1), ("rot", 2, 1), ("rot", 3, 0),
+    ("rot", 3, 1), ("sq", 1), ("sq", 2), ("sq", 0), ("sq", 3), ("spr", 1), ("spr", 2), ("spr", 3), ("spr", 0),
+    ("mid", 1), ("mid", 2), ("mid", 3), ("mid", 0), ("fin", 1), ("fin", 2), ("fin", 3), ("fin", 0),
 )
 
 

time: 105 us -> 109 us (1.038)
  Pallas kernels: 103 us -> 107 us
    pallas_call x1, Pallas kernels: 103 us -> 107 us  [shards(): pl.pallas_call(kernel, name='eigenvalues', out_shape=jax.ShapeDtypeStruct...]
where the time goes in v7:
time: 109 us
  Pallas kernels  107 us (98%)
  local copies, waits for them, and re-layouts  1.67 us (2%)
    pallas_call x1, Pallas kernels, shards(): pl.pallas_call(kernel, name='eigenvalues', out_shape=jax.ShapeDtypeStruct...  107 us

profile of v7, /device:TPU:1, one launch (start us, length us, event | category | flops | bytes accessed | tf_op | source)
XLA Modules:
  0.0 109.1 jit_solution(15777087649031913263)
XLA Ops:
  0.0 107.4 %eigenvalues.1 = f32[512,128]{1,0:T(8,128)} custom-call(bf16[512,128]{1,0:T(8,128)(2,1)} %acts.1, bf16[512,512]{1,0:T(8,128)(2,1)} %grads.1, bf16[512,8192]{1,0:T(8,128)(2,1)} %bout.1, bf16[128,2048]{1,0:T(8,128)(2,1)} %bin_.1, s32[32]{0:T(128)} %slot_seq.1, s32[32]{0:T(128)} %seq_len.1), custom_call_target="tpu_custom_call" | custom-call | flops 10737418240 | bytes 12582912 | tf_op jit(solution)/shard_map/eigenvalues/pallas_call | solution.py:347
  107.4 1.7 %copy.8 = f32[512,128]{1,0:T(8,128)} copy(f32[512,128]{1,0:T(8,128)} %eigenvalues.1) | data formatting | bytes 524288

commit v8 on v7

--- a/solution.py
+++ b/solution.py
@@ -12,15 +12,15 @@
 GROUPS = ((0, 1), (1, 3), (3, 5), (5, 8))
 QS = 4
 WORK = (
-    ("py", 0), ("py", 2), ("bhop", 1), ("py", 1), ("ahop", 0, 1), ("bw", 1), ("bhop", 2), ("ay",), ("px", 0),
-    ("g",), ("py", 3), ("px", 2), ("bw", 2), ("bhop", 3), ("aw", 0, 1), ("ahop", 0, 2), ("px", 1), ("pr", 0),
-    ("bw", 3), ("bhop", 4), ("ayw",), ("ahop", 1, 1), ("pr", 2), ("bw", 4), ("aw", 0, 2), ("pr", 1),
-    ("ahop", 0, 3), ("pc", 2), ("aw", 1, 1), ("pc", 0), ("by",), ("ahop", 1, 2), ("bs", 0), ("pc", 1),
-    ("aw", 0, 3), ("ahop", 0, 4), ("pw", 0), ("aw", 1, 2), ("ahop", 1, 3), ("gw",), ("st", 0, 0),
-    ("aw", 0, 4), ("st", 0, 1), ("px", 3), ("pw", 2), ("br", 0), ("pw", 1), ("aw", 1, 3), ("ahop", 1, 4),
-    ("st", 1, 0), ("pr", 3), ("st", 1, 1), ("byw",), ("bs", 1), ("rot", 1, 0), ("st", 2, 0), ("bl", 0),
-    ("aw", 1, 4), ("st", 2, 1), ("pc", 3), ("rot", 0, 0), ("pw", 3), ("br", 1), ("st", 3, 0), ("rot", 1, 1),
-    ("rot", 0, 1), ("st", 3, 1), ("own",), ("rot", 2, 0), ("bl", 1), ("rot", 2, 1), ("rot", 3, 0),
+    ("py", 0), ("bhop", 1), ("py", 1), ("ahop", 0, 1), ("py", 2), ("ay",), ("bw", 1), ("bhop", 2), ("px", 0),
+    ("px", 1), ("g",), ("bw", 2), ("bhop", 3), ("aw", 0, 1), ("ahop", 0, 2), ("px", 2), ("bw", 3),
+    ("bhop", 4), ("pr", 0), ("ayw",), ("ahop", 1, 1), ("pr", 1), ("py", 3), ("pr", 2), ("aw", 0, 2),
+    ("ahop", 0, 3), ("bw", 4), ("bs", 0), ("by",), ("aw", 1, 1), ("pc", 0), ("ahop", 1, 2), ("pw", 0),
+    ("aw", 0, 3), ("ahop", 0, 4), ("gw",), ("st", 0, 0), ("pc", 1), ("st", 0, 1), ("px", 3), ("aw", 1, 2),
+    ("ahop", 1, 3), ("pw", 1), ("st", 1, 0), ("pc", 2), ("pr", 3), ("st", 1, 1), ("byw",), ("bs", 1),
+    ("br", 0), ("aw", 1, 3), ("aw", 0, 4), ("pw", 2), ("st", 2, 0), ("ahop", 1, 4), ("rot", 0, 0), ("pc", 3),
+    ("pw", 3), ("st", 2, 1), ("rot", 2, 0), ("st", 3, 0), ("br", 1), ("rot", 1, 0), ("own",), ("aw", 1, 4),
+    ("rot", 1, 1), ("st", 3, 1), ("bl", 0), ("rot", 2, 1), ("rot", 0, 1), ("bl", 1), ("rot", 3, 0),
     ("rot", 3, 1), ("sq", 1), ("sq", 2), ("sq", 0), ("sq", 3), ("spr", 1), ("spr", 2), ("spr", 3), ("spr", 0),
     ("mid", 1), ("mid", 2), ("mid", 3), ("mid", 0), ("fin", 1), ("fin", 2), ("fin", 3), ("fin", 0),
 )

time: 109 us -> 108 us (level)
  no operation moved by 1% of the time
where the time goes in v8:
time: 108 us
  Pallas kernels  106 us (98%)
  local copies, waits for them, and re-layouts  1.67 us (2%)
    pallas_call x1, Pallas kernels, shards(): pl.pallas_call(kernel, name='eigenvalues', out_shape=jax.ShapeDtypeStruct...  106 us

profile of v8, /device:TPU:1, one launch (start us, length us, event | category | flops | bytes accessed | tf_op | source)
XLA Modules:
  0.0 108.0 jit_solution(13544263937425363082)
XLA Ops:
  0.0 106.3 %eigenvalues.1 = f32[512,128]{1,0:T(8,128)} custom-call(bf16[512,128]{1,0:T(8,128)(2,1)} %acts.1, bf16[512,512]{1,0:T(8,128)(2,1)} %grads.1, bf16[512,8192]{1,0:T(8,128)(2,1)} %bout.1, bf16[128,2048]{1,0:T(8,128)(2,1)} %bin_.1, s32[32]{0:T(128)} %slot_seq.1, s32[32]{0:T(128)} %seq_len.1), custom_call_target="tpu_custom_call" | custom-call | flops 10737418240 | bytes 12582912 | tf_op jit(solution)/shard_map/eigenvalues/pallas_call | solution.py:347
  106.3 1.7 %copy.8 = f32[512,128]{1,0:T(8,128)} copy(f32[512,128]{1,0:T(8,128)} %eigenvalues.1) | data formatting | bytes 524288
